TPU v7x, 128 devices: a whole 4x4x4 slice. The times are simulated.
128 devices in a mesh: mod: 4 (over y_lo, core), dp: 16 (over x, z), tp: 2 (over y_hi).
Axes of the slice: x: 4, y: 4 (y_hi: 2, y_lo: 2; y = y_hi * 2 + y_lo), z: 4, core: 2. Of those that a mesh axis runs over, the one named last changes fastest.
Arguments:
- tokens: bfloat16 [128, 257, 1280], P(('mod', 'dp')), may hold values from -133 to 133
- w_qkv: bfloat16 [1280, 3, 1280], P('mod', None, 'tp'), may hold values from -0.15625 to 0.15625
- w_out: bfloat16 [1280, 1280], P('mod', 'tp'), may hold values from -0.15625 to 0.15625
- w_proj: bfloat16 [1280, 1024], P('mod'), may hold values from -0.15625 to 0.15625
- other_emb: bfloat16 [128, 1024], P(('mod', 'dp')), may hold values from -6 to 6
Outputs:
- loss: float32 [4], P('mod')
- grad_tokens: bfloat16 [128, 257, 1280], P(('mod', 'dp'), None, 'tp')
- grad_qkv: float32 [1280, 3, 1280], P(('mod', 'dp'), None, 'tp')
- grad_out: float32 [1280, 1280], P(('mod', 'dp'), 'tp')
- grad_proj: float32 [1280, 1024], P(('mod', 'dp'))
- grad_other: bfloat16 [128, 1024], P(('mod', 'dp'))
All inputs are finite; a program needn't handle non-finite values.
Results may differ from a plain program's by a relative error of at most 0.02.
Values may be sent and summed in bfloat16 or wider, within the bound.
A program may use at most 128 MiB of HBM per device.

v0:
```python
import jax
import jax.numpy as jnp
from jax import lax
from jax.sharding import PartitionSpec as P

HEAD_DIM = 80


EPSILON = 1e-06
LOGIT_SCALE = 1.0 / 0.07


def layer_stats(values):
    centered = values - jnp.mean(values, axis=-1, keepdims=True)
    inv_std = lax.rsqrt(jnp.mean(centered * centered, axis=-1, keepdims=True) + EPSILON)
    return (centered * inv_std, inv_std)


def layer_back(grad_in, normed, inv_std):
    mean_grad = jnp.mean(grad_in, axis=-1, keepdims=True)
    mean_cross = jnp.mean(grad_in * normed, axis=-1, keepdims=True)
    return inv_std * (grad_in - mean_grad - normed * mean_cross)


def contract_first(left, right):
    return lax.dot_general(
        left, right, (((0,), (0,)), ((), ())), preferred_element_type=jnp.float32
    )


def contract_last(left, right):
    return lax.dot_general(
        left, right, (((1,), (1,)), ((), ())), preferred_element_type=jnp.float32
    )


def local(tokens, w_qkv, w_out, w_proj, other_emb):
    img_rows, tok_count, model_width = tokens.shape
    qkv_full, out_full, proj_full = (
        lax.all_gather(w_qkv, "mod", axis=0, tiled=True),
        lax.all_gather(w_out, "mod", axis=0, tiled=True),
        lax.all_gather(w_proj, "mod", axis=0, tiled=True),
    )
    local_cols = qkv_full.shape[2]
    head_count = local_cols // HEAD_DIM
    scale_dot = HEAD_DIM ** (-0.5)
    normed, inv_std = layer_stats(tokens.astype(jnp.float32))
    normed_b = normed.astype(jnp.bfloat16)
    flat_rows = normed_b.reshape(img_rows * tok_count, model_width)
    kv_weight = qkv_full[:, 1:3, :].reshape(model_width, 2 * local_cols)
    key_value = jnp.dot(flat_rows, kv_weight, preferred_element_type=jnp.float32).astype(
        jnp.bfloat16
    )
    key_rows = key_value[:, :local_cols].reshape(img_rows, tok_count, head_count, HEAD_DIM)
    value_rows = key_value[:, local_cols:].reshape(img_rows, tok_count, head_count, HEAD_DIM)
    query_b = jnp.dot(normed_b[:, 0], qkv_full[:, 0, :], preferred_element_type=jnp.float32).astype(
        jnp.bfloat16
    )
    query_heads_b = query_b.reshape(img_rows, head_count, HEAD_DIM)
    scores = (
        jnp.einsum("nhd,nthd->nht", query_heads_b, key_rows, preferred_element_type=jnp.float32)
        * scale_dot
    )
    expo_attn = jnp.exp(scores)
    soft = expo_attn / jnp.sum(expo_attn, axis=-1, keepdims=True)
    soft_b = soft.astype(jnp.bfloat16)
    context = jnp.einsum("nht,nthd->nhd", soft_b, value_rows, preferred_element_type=jnp.float32)
    context_b = context.astype(jnp.bfloat16).reshape(img_rows, local_cols)
    attn_part = contract_last(context_b, out_full)
    attn_full = lax.psum(attn_part, "tp")
    hidden_row = tokens[:, 0].astype(jnp.float32) + attn_full
    head_normed, head_inv = layer_stats(hidden_row)
    head_b = head_normed.astype(jnp.bfloat16)
    proj_rows = jnp.dot(head_b, proj_full, preferred_element_type=jnp.float32)
    proj_inv = lax.rsqrt(jnp.sum(proj_rows * proj_rows, axis=-1, keepdims=True) + EPSILON)
    embed = proj_rows * proj_inv
    embed_b = embed.astype(jnp.bfloat16)
    other_f = other_emb.astype(jnp.float32)
    other_inv = lax.rsqrt(jnp.sum(other_f * other_f, axis=-1, keepdims=True) + EPSILON)
    other_unit = other_f * other_inv
    other_b = other_unit.astype(jnp.bfloat16)
    pair_all = lax.all_gather(other_b, "dp", axis=0, tiled=True)
    pair_total = pair_all.shape[0]
    logits = LOGIT_SCALE * contract_last(embed_b, pair_all)
    expo = jnp.exp(logits)
    row_total = jnp.sum(expo, axis=1)
    col_part = jnp.sum(expo, axis=0)
    offset = lax.axis_index("dp") * img_rows
    own_block = lax.dynamic_slice_in_dim(logits, offset, img_rows, 1)
    diag_sum = jnp.sum(jnp.diagonal(own_block))
    loss_piece = 0.5 * jnp.sum(jnp.log(row_total)) - diag_sum
    col_total, piece_total = lax.psum((col_part, loss_piece), "dp")
    loss = ((piece_total + 0.5 * jnp.sum(jnp.log(col_total))) / pair_total).reshape(1)
    match_mask = jnp.arange(pair_total)[None, :] == (offset + jnp.arange(img_rows))[:, None]
    grad_logit = 0.5 / pair_total * (expo / row_total[:, None] + expo / col_total[None, :])
    grad_logit = grad_logit - jnp.where(match_mask, 1.0 / pair_total, 0.0)
    grad_logit_b = grad_logit.astype(jnp.bfloat16)
    d_embed = LOGIT_SCALE * jnp.dot(grad_logit_b, pair_all, preferred_element_type=jnp.float32)
    pair_term = contract_first(grad_logit_b, embed_b)
    d_unit = LOGIT_SCALE * lax.psum_scatter(
        pair_term.astype(jnp.bfloat16), "dp", scatter_dimension=0, tiled=True
    ).astype(jnp.float32)
    d_proj = (d_embed - embed * jnp.sum(embed * d_embed, axis=-1, keepdims=True)) * proj_inv
    d_proj_b = d_proj.astype(jnp.bfloat16)
    grad_other = (
        (d_unit - other_unit * jnp.sum(other_unit * d_unit, axis=-1, keepdims=True)) * other_inv
    ).astype(jnp.bfloat16)
    d_head = contract_last(d_proj_b, proj_full)
    d_hidden = layer_back(d_head, head_normed, head_inv)
    d_hidden_b = d_hidden.astype(jnp.bfloat16)
    d_context = jnp.dot(d_hidden_b, out_full, preferred_element_type=jnp.float32)
    d_context_b = d_context.astype(jnp.bfloat16).reshape(img_rows, head_count, HEAD_DIM)
    d_soft = jnp.einsum(
        "nhd,nthd->nht", d_context_b, value_rows, preferred_element_type=jnp.float32
    )
    d_score = soft * (d_soft - jnp.sum(soft * d_soft, axis=-1, keepdims=True))
    d_score_b = d_score.astype(jnp.bfloat16)
    d_query = (
        jnp.einsum("nht,nthd->nhd", d_score_b, key_rows, preferred_element_type=jnp.float32)
        * scale_dot
    )
    d_query_b = d_query.astype(jnp.bfloat16).reshape(img_rows, local_cols)
    query_heads = query_heads_b.astype(jnp.float32)
    d_key = jnp.einsum("nht,nhd->nthd", d_score, query_heads) * scale_dot
    d_value = jnp.einsum(
        "nht,nhd->nthd", soft_b.astype(jnp.float32), d_context_b.astype(jnp.float32)
    )
    kv_grad_b = jnp.concatenate(
        [
            d_key.reshape(img_rows * tok_count, local_cols),
            d_value.reshape(img_rows * tok_count, local_cols),
        ],
        axis=1,
    ).astype(jnp.bfloat16)
    class_rows = normed_b[:, 0]
    grad_rows = model_width // lax.axis_size(("mod", "dp"))
    query_term = contract_first(class_rows, d_query_b)
    kv_term = contract_first(flat_rows, kv_grad_b)
    out_term = contract_first(d_hidden_b, context_b)
    proj_term = contract_first(head_b, d_proj_b)
    summed = lax.psum_scatter(
        jnp.concatenate([query_term, kv_term, out_term, proj_term], axis=1),
        ("mod", "dp"),
        scatter_dimension=0,
        tiled=True,
    )
    grad_qkv = summed[:, : 3 * local_cols].reshape(grad_rows, 3, local_cols)
    grad_out = summed[:, 3 * local_cols : 4 * local_cols]
    grad_proj = summed[:, 4 * local_cols :]
    d_normed = contract_last(kv_grad_b, kv_weight).reshape(img_rows, tok_count, model_width)
    d_normed = d_normed.at[:, 0].add(contract_last(d_query_b, qkv_full[:, 0, :]))
    half_width = model_width // lax.axis_size("tp")
    half_start = lax.axis_index("tp") * half_width
    full_grad = lax.psum(d_normed.astype(jnp.bfloat16), "tp").astype(jnp.float32)
    token_grad = layer_back(full_grad, normed, inv_std)
    token_grad = token_grad.at[:, 0].add(d_hidden)
    grad_tokens = lax.dynamic_slice_in_dim(token_grad, half_start, half_width, 2).astype(
        jnp.bfloat16
    )
    return (loss, grad_tokens, grad_qkv, grad_out, grad_proj, grad_other)


def solution(mesh):
    placed = (
        P(("mod", "dp"), None, None),
        P("mod", None, "tp"),
        P("mod", "tp"),
        P("mod", None),
        P(("mod", "dp"), None),
    )
    return jax.shard_map(
        local,
        mesh=mesh,
        in_specs=placed,
        out_specs=(
            P("mod"),
            P(("mod", "dp"), None, "tp"),
            P(("mod", "dp"), None, "tp"),
            P(("mod", "dp"), "tp"),
            P(("mod", "dp"), None),
            P(("mod", "dp"), None),
        ),
        check_vma=False,
    )
```

profile of v0, /device:TPU:1, one launch (start us, length us, event | category | flops | bytes accessed | tf_op | source)
XLA Modules:
  0.0 993.8 jit_solution(14594691595650011500)
XLA Ops:
  11.5 20.3 %all-gather = bf16[16,2,1024]{2,1,0:T(2,128)(2,1)S(1)} all-gather(bf16[1,2,1024]{2,1,0:T(2,128)(2,1)S(1)} %fusion.33), channel_id=1, replica_groups=mesh['mod'=4,'dp'=16,'tp'=2] {'dp'}, dimensions={0}, use_global_device_ids=true | all-gather | bytes 69632 | tf_op jit(solution)/shard_map/all_gather | solution.py:82
  31.9 1.1 convert_reduce_fusion.1
  33.0 1.9 fusion.2
  35.6 1.7 fusion.8
  37.3 1.1 copy-done.5
  38.5 1.4 reshape.185
  39.9 25.9 %all-gather.5.cloned.1.call-done = bf16[1280,3,640]{2,0,1:T(8,128)(2,1)} async-done(((bf16[320,3,640]{2,0,1:T(8,128)(2,1)}), bf16[1280,3,640]{2,0,1:T(8,128)(2,1)}) %all-gather.5.cloned.1.call-update) | async-done | bytes 4915216 | tf_op jit(solution)/shard_map/all_gather | solution.py:40
  65.9 1.8 fusion.18
  67.7 4.1 fusion.56
  72.1 1.0 copy-done.12
  73.2 1.9 convolution_convert_fusion
  76.0 1.1 reshape.188
  77.1 2.3 reshape.187
  82.3 11.5 %all-gather.7.cloned.1.call-done = bf16[1280,640]{1,0:T(8,128)(2,1)} async-done(((bf16[320,640]{1,0:T(8,128)(2,1)}), bf16[1280,640]{1,0:T(8,128)(2,1)}) %all-gather.7.cloned.1.call-update) | async-done | bytes 1638416 | tf_op jit(solution)/shard_map/all_gather | solution.py:41
  93.8 2.0 fusion.58
  95.7 8.8 psum.28
  104.9 24.9 %all-gather.9.cloned.1.call-done = bf16[1280,1024]{1,0:T(8,128)(2,1)} async-done(((bf16[320,1024]{1,0:T(8,128)(2,1)}), bf16[1280,1024]{1,0:T(8,128)(2,1)}) %all-gather.9.cloned.1.call-update) | async-done | bytes 2621456 | tf_op jit(solution)/shard_map/all_gather | solution.py:42
  129.8 2.3 multiply_reduce_fusion.8
  135.7 34.0 %all-reduce.2 = (f32[]{:T(128)}, f32[32]{0:T(128)S(1)}) all-reduce(f32[]{:T(128)S(6)} %sub.62, f32[32]{0:T(128)S(1)} %get-tuple-element.52), channel_id=1, replica_groups=mesh['mod'=4,'dp'=16,'tp'=2] {'dp'}, use_global_device_ids=true, to_apply=%region_11.12 | all-reduce | flops 33 | bytes 264 | tf_op jit(solution)/shard_map/psum | solution.py:92
  170.7 1.6 convolution_convert_fusion.1
  172.3 16.4 %copy.25 = bf16[1280,2,640]{2,1,0:T(2,128)(2,1)} copy(bf16[1280,2,640]{2,0,1:T(8,128)(2,1)} %get-tuple-element.58) | data formatting | bytes 6553600 | tf_op jit(solution)/shard_map/slice | solution.py:50
  188.7 8.2 reshape.213
  196.9 3.3 fusion.38
  200.2 1.7 fusion.55
  201.9 2.4 fusion.35
  204.7 3.0 multiply_reduce_fusion.1
  209.6 1.9 concatenate.25
  211.5 1.6 fusion.19
  213.1 1.9 concatenate.24
  215.0 4.3 fusion.10
  219.3 3.0 copy.27
  222.3 3.1 fusion.34
  225.4 2.6 fusion.7
  228.0 1.8 reshape.196
  229.8 1.8 reshape.195
  231.6 3.8 convert_element_type.95
  235.8 4.1 fusion.14
  239.9 8.9 pad_maximum_fusion
  253.9 37.4 %all-reduce.11.cloned.1.call-done = bf16[32,1024]{1,0:T(8,128)(2,1)} async-done(((bf16[32,1024]{1,0:T(8,128)(2,1)}), bf16[32,1024]{1,0:T(8,128)(2,1)}) %all-reduce.11.cloned.1.call-update) | async-done | bytes 65552
  292.3 1.4 fusion.32
  293.7 54.7 %all-reduce.7.cloned.1.call-done = bf16[2,257,1280]{2,0,1:T(2,128)(2,1)} async-done(((bf16[2,257,1280]{2,0,1:T(2,128)(2,1)}), bf16[2,257,1280]{2,0,1:T(2,128)(2,1)}) %all-reduce.7.cloned.1.call-update) | async-done | bytes 1315856 | tf_op jit(solution)/shard_map/psum | solution.py:154
  348.4 8.2 convert_reduce_fusion
  356.7 3.0 fusion.4
  359.8 1.3 dynamic-slice_convert_fusion
  361.1 617.5 %all-reduce.9.cloned.1.call-done = f32[1280,3584]{0,1:T(8,128)} async-done(((f32[1280,3584]{0,1:T(8,128)}), f32[1280,3584]{0,1:T(8,128)}) %all-reduce.9.cloned.1.call-update) | async-done | bytes 18350096
  978.7 1.2 dynamic-slice.21
  980.7 1.4 dynamic-slice.22
  983.0 1.9 constant_dynamic-slice_fusion.1
  (106 shorter events, 21.8 us)
Async XLA Ops:
  7.2 24.7 %copy-start = (bf16[2,257,1280]{2,0,1:T(2,128)(2,1)S(1)}, bf16[2,257,1280]{2,0,1:T(2,128)(2,1)}, u32[]{:S(2)}) copy-start(bf16[2,257,1280]{2,0,1:T(2,128)(2,1)} %param.9) | copy-start | bytes 3947524
  7.2 58.7 %all-gather.5.cloned.1.call-start = ((), (), s32[]{:S(2)}) async-start(), calls=%async_computation | async-start | bytes 6144000 | tf_op jit(solution)/shard_map/all_gather | solution.py:40
  7.9 85.9 %all-gather.7.cloned.1.call-start = ((), (), s32[]{:S(2)}) async-start(), calls=%async_computation.1 | async-start | bytes 2048000 | tf_op jit(solution)/shard_map/all_gather | solution.py:41
  8.7 121.2 %all-gather.9.cloned.1.call-start = ((), (), s32[]{:S(2)}) async-start(), calls=%async_computation.2 | async-start | bytes 3276800 | tf_op jit(solution)/shard_map/all_gather | solution.py:42
  9.4 282.0 %all-reduce.11.cloned.1.call-start = ((), (), s32[]{:S(2)}) async-start(), calls=%async_computation.5 | async-start | bytes 131072
  33.0 1.9 copy-start.7
  34.9 0.7 copy-start.9
  37.3 1.1 copy-start.5
  71.8 1.3 copy-start.12
  80.8 0.7 copy-start.15
  132.2 64.8 %copy-start.18 = (f32[2]{0:T(128)}, f32[2]{0:T(128)S(1)}, u32[]{:S(2)}) copy-start(f32[2]{0:T(128)S(1)} %add_rsqrt_fusion.2) | copy-start | bytes 28
  132.5 1.3 copy-start.23
  169.7 19.0 %copy-start.21 = (f32[32]{0:T(128)}, f32[32]{0:T(128)S(1)}, u32[]{:S(2)}) copy-start(f32[32]{0:T(128)S(1)} %get-tuple-element.55) | copy-start | bytes 388
  196.9 3.3 copy-start.3
  200.2 4.1 copy-start.11
  204.7 3.0 copy-start.14
  207.7 1.9 copy-start.4
  209.3 139.1 %all-reduce.7.cloned.1.call-start = ((), (), s32[]{:S(2)}) async-start(), calls=%async_computation.3 | async-start | bytes 2631680 | tf_op jit(solution)/shard_map/psum | solution.py:154
  231.6 4.2 copy-start.13
  231.6 4.2 copy-start.16
  235.5 743.2 %all-reduce.9.cloned.1.call-start = ((), (), s32[]{:S(2)}) async-start(), calls=%async_computation.4 | async-start | bytes 36700160
  235.8 4.1 copy-start.1
  235.8 4.1 copy-start.2
  248.9 0.7 copy-start.20
  248.9 1.2 copy-start.19
  248.9 3.1 copy-start.22
  248.9 42.5 %copy-start.17 = (bf16[2,1024]{1,0:T(2,128)(2,1)S(1)}, bf16[2,1024]{1,0:T(2,128)(2,1)}, u32[]{:S(2)}) copy-start(bf16[2,1024]{1,0:T(2,128)(2,1)} %param.13) | copy-start | bytes 12292
  248.9 99.5 %copy-start.8 = (f32[2,257]{0,1:T(8,128)S(1)}, f32[2,257]{0,1:T(8,128)}, u32[]{:S(2)}) copy-start(f32[2,257]{0,1:T(8,128)} %copy-done.7) | copy-start | bytes 6172
  248.9 99.5 %copy-start.10 = (f32[2,257]{0,1:T(8,128)S(1)}, f32[2,257]{0,1:T(8,128)}, u32[]{:S(2)}) copy-start(f32[2,257]{0,1:T(8,128)} %copy-done.9) | copy-start | bytes 6172
  348.4 8.3 copy-start.6
Sparse Core Ops, SparseCore 0:
  9.7 56.1 all-gather.4
  67.5 26.1 all-gather.6
  95.4 34.3 all-gather.8
  209.5 81.8 all-reduce.10
  293.8 54.5 all-reduce.6
  350.8 627.8 all-reduce.8
where the time goes:
time: 1010 us; the launch traced here: 994 us
  waiting for transfers between devices  774 us (77%)
  blocking collectives  63.1 us (6%)
  local copies, waits for them, and re-layouts  60 us (6%)
  other arithmetic  43.8 us (4%)
  matrix products  32.6 us (3%)
  between operations  19.5 us (2%)
    unnamed x8, waiting for transfers between devices  657 us
    psum x1, waiting for transfers between devices, local(): lax.psum(d_normed.astype(jnp.bfloat16), 'tp').astype(jnp.float32)  54.7 us
    psum x1, blocking collectives, local(): col_total, piece_total = lax.psum((col_part, loss_piece), 'dp')  34 us
    all_gather x1, waiting for transfers between devices, local(): lax.all_gather(w_qkv, 'mod', axis=0, tiled=True)  25.9 us
    all_gather x1, waiting for transfers between devices, local(): lax.all_gather(w_proj, 'mod', axis=0, tiled=True)  24.9 us
    slice x2, local copies, waits for them, and re-layouts, local(): kv_weight = qkv_full[:, 1:3, :].reshape(model_width, 2 * local_cols)  20.5 us
    all_gather x1, blocking collectives, local(): pair_all = lax.all_gather(other_b, 'dp', axis=0, tiled=True)  20.3 us
  transfers between devices with their start and end apart: 6, of which 6 were waited for; matrix products, arithmetic and copies ran while one was open for 8% of the time, Pallas kernels for 0%

commit v1 on v0

v1 whole, which is shorter than its diff:
```python
import functools

import jax
import jax.numpy as jnp
from jax import lax
from jax.experimental import pallas as pl
from jax.experimental.pallas import tpu as pltpu
from jax.sharding import PartitionSpec as P

HEAD_DIM = 80
EPSILON = 1e-06
LOGIT_SCALE = 1.0 / 0.07
MESH = pl.DeviceIdType.MESH
F32 = jnp.float32
BF16 = jnp.bfloat16

N_MOD, N_DP, N_TP = 4, 16, 2
IMGS = 2
GROUP = N_MOD * IMGS
HEADS = 8
TOK = 257
ROWS = IMGS * TOK
PAD_ROWS = 528
CHUNK = 176
D = 1280
HALF = D // 2
SLICE = D // N_MOD
OUT_ROWS = SLICE // N_DP
E = 1024
PAIRS = 32
ALL = GROUP * N_DP
SCALE = HEAD_DIM**-0.5


def dot(a, b):
    return jnp.dot(a, b, preferred_element_type=F32)


def dot_nt(a, b):
    return lax.dot_general(a, b, (((1,), (1,)), ((), ())), preferred_element_type=F32)


def dot_tn(a, b):
    return lax.dot_general(a, b, (((0,), (0,)), ((), ())), preferred_element_type=F32)


def split_high_low(v):
    high = v.astype(BF16)
    low = (v - high.astype(F32)).astype(BF16)
    return jnp.concatenate([high.astype(F32), low.astype(F32)], axis=0).astype(BF16)


def fold_halves(v):
    k = v.shape[1] // 2
    return jnp.concatenate([v[:, :k], v[:, k:]], axis=0).astype(BF16)


def unfold_halves(v):
    wide = v.astype(F32)
    return jnp.concatenate(
        [wide[:, :8].reshape(ALL, -1), wide[:, 8:].reshape(ALL, -1)], axis=1
    )


def head_mask():
    lane = lax.broadcasted_iota(jnp.int32, (HEADS, HALF), 1)
    head = lax.broadcasted_iota(jnp.int32, (HEADS, HALF), 0) * HEAD_DIM
    return (lane >= head) & (lane < head + HEAD_DIM)


def expand_heads(v, mask):
    return jnp.concatenate(
        [jnp.where(mask, v[b : b + 1], 0.0) for b in range(GROUP)], axis=0
    ).astype(BF16)


def collapse_heads(v, mask):
    return jnp.concatenate(
        [
            jnp.sum(
                jnp.where(mask, v[b * HEADS : (b + 1) * HEADS], 0.0), axis=0, keepdims=True
            )
            for b in range(GROUP)
        ],
        axis=0,
    )


def row_sum(v):
    return jnp.sum(v, axis=-1, keepdims=True)


def kernel(
    x_ref, wqkv_ref, wout_ref, wproj_ref, other_ref,
    loss_ref, gtok_ref, gqkv_ref, gout_ref, gproj_ref, gother_ref,
    xn_ref, mu_ref, inv_ref, grad_ref, dn_ref, dn0_ref, unit_ref, qbd_ref, dbd_ref,
    s_cls, d_cls, s_oth, d_oth, s_q, d_q, s_kq, d_kq, s_w, d_w, s_ctx, d_ctx, s_att, d_att,
    s_prj, d_prj, s_hs, d_hs, s_dh, d_dh, s_vd, d_vd, s_u, d_u, s_dq, d_dq, s_cg, d_cg,
    s_sc, d_sc, s_kv, d_kv,
    f_oth, g_oth, f_emb, g_emb, f_dpr, g_dpr, f_qc, g_qc, f_dd, g_dd, f_ea, g_ea, f_la, g_la,
    mod_send, mod_recv, all_send, all_recv, tp_send, tp_recv, dp_send, dp_recv,
):
    m, d, t = lax.axis_index("mod"), lax.axis_index("dp"), lax.axis_index("tp")
    me = t * N_MOD + m

    barrier = pltpu.get_barrier_semaphore()
    for k in range(1, N_MOD):
        pl.semaphore_signal(
            barrier, 1, device_id=(lax.rem(m + k, N_MOD), d, t), device_id_type=MESH
        )
    for k in range(N_MOD):
        pl.semaphore_signal(
            barrier, 1, device_id=(lax.rem(m + k, N_MOD), d, 1 - t), device_id_type=MESH
        )

    def greet(k, carry):
        pl.semaphore_signal(
            barrier, 1, device_id=(m, lax.rem(d + k, N_DP), t), device_id_type=MESH
        )
        return carry

    lax.fori_loop(1, N_DP, greet, 0)

    def mod_copy(n, k, src, dst, slot):
        peer = lax.rem(m + k, N_MOD)
        return pltpu.make_async_remote_copy(
            src(peer),
            dst.at[m if slot is None else peer],
            mod_send.at[n, k],
            mod_recv.at[n, m if slot is None else peer],
            device_id=(peer, d, t),
            device_id_type=MESH,
        )

    def mod_start(n, src, dst):
        for k in range(1, N_MOD):
            mod_copy(n, k, src, dst, None).start()

    def mod_wait(n, src, dst):
        for k in range(1, N_MOD):
            mod_copy(n, k, src, dst, 0).wait_recv()

    def mod_end(n, src, dst):
        for k in range(1, N_MOD):
            mod_copy(n, k, src, dst, None).wait_send()

    def all_copy(n, k, src, dst, landing):
        peer_m = lax.rem(m + k, N_MOD)
        peer_t = t if k < N_MOD else 1 - t
        slot = peer_t * N_MOD + peer_m if landing else me
        return pltpu.make_async_remote_copy(
            src,
            dst.at[slot],
            all_send.at[n, k],
            all_recv.at[n, slot],
            device_id=(peer_m, d, peer_t),
            device_id_type=MESH,
        )

    def all_start(n, src, dst):
        for k in range(1, 2 * N_MOD):
            all_copy(n, k, src, dst, False).start()

    def all_wait(n, src, dst):
        for k in range(1, 2 * N_MOD):
            all_copy(n, k, src, dst, True).wait_recv()

    def all_end(n, src, dst):
        for k in range(1, 2 * N_MOD):
            all_copy(n, k, src, dst, False).wait_send()

    def dp_copy(n, k, src, dst, landing):
        peer = lax.rem(d + k, N_DP)
        slot = peer if landing else d
        return pltpu.make_async_remote_copy(
            src(peer),
            dst.at[slot],
            dp_send.at[n, k],
            dp_recv.at[n, slot],
            device_id=(m, peer, t),
            device_id_type=MESH,
        )

    def dp_start(n, src, dst):
        def body(k, carry):
            dp_copy(n, k, src, dst, False).start()
            return carry

        lax.fori_loop(1, N_DP, body, 0)

    def dp_wait(n, src, dst):
        def body(k, carry):
            dp_copy(n, k, src, dst, True).wait_recv()
            return carry

        lax.fori_loop(1, N_DP, body, 0)

    def dp_end(n, src, dst):
        def body(k, carry):
            dp_copy(n, k, src, dst, False).wait_send()
            return carry

        lax.fori_loop(1, N_DP, body, 0)

    def tp_copy(n, src, dst):
        return pltpu.make_async_remote_copy(
            src, dst, tp_send.at[n], tp_recv.at[n], device_id=(m, d, 1 - t), device_id_type=MESH
        )

    def whole(ref):
        return lambda peer: ref

    def part(ref):
        return lambda peer: ref.at[peer]

    row8 = lax.broadcasted_iota(jnp.int32, (GROUP, 1), 0)
    mask = head_mask()

    def place(v):
        return jnp.where(row8 == 2 * m, v[0:1], jnp.where(row8 == 2 * m + 1, v[1:2], 0.0))

    def own_rows(v):
        first = jnp.sum(jnp.where(row8 == 2 * m, v, 0.0), axis=0, keepdims=True)
        second = jnp.sum(jnp.where(row8 == 2 * m + 1, v, 0.0), axis=0, keepdims=True)
        return jnp.where(row8 == 0, first, jnp.where(row8 == 1, second, 0.0))

    def normalise(c):
        at = pl.ds(c * CHUNK, CHUNK)
        x = x_ref[at, :].astype(F32)
        mu = row_sum(x) * (1.0 / D)
        x = x - mu
        inv = lax.rsqrt(row_sum(x * x) * (1.0 / D) + EPSILON)
        xn_ref[at, :] = (x * inv).astype(BF16)
        mu_ref[at, :] = mu
        inv_ref[at, :] = inv

    def windows(dst, v):
        wide = jnp.concatenate([v, jnp.zeros((v.shape[0], 192), F32)], axis=1)
        for k in range(N_DP):
            dst[k] = wide[:, k * OUT_ROWS : k * OUT_ROWS + 128].astype(BF16)

    x8 = x_ref[0:16, :].astype(F32)[0:8]
    mu8 = row_sum(x8) * (1.0 / D)
    c8 = x8 - mu8
    n8 = c8 * lax.rsqrt(row_sum(c8 * c8) * (1.0 / D) + EPSILON)
    cls = jnp.concatenate([place(n8), place(x8)], axis=0)
    for p in range(N_MOD):
        s_cls[p] = cls[:, p * SLICE : (p + 1) * SLICE]
    d_cls[m] = s_cls[m]
    oth = place(other_ref[...].astype(F32))
    s_oth[...] = oth
    d_oth[m] = oth
    pl.semaphore_wait(barrier, N_MOD - 1 + N_MOD + N_DP - 1)
    mod_start(0, part(s_cls), d_cls)
    mod_start(1, whole(s_oth), d_oth)
    normalise(0)
    mod_wait(0, part(s_cls), d_cls)
    cls = d_cls[0] + d_cls[1] + d_cls[2] + d_cls[3]
    n0, x0 = cls[0:8], cls[8:16]

    qp = dot(n0.astype(BF16), wqkv_ref[0])
    s_q[...] = qp
    d_q[m] = qp
    mod_start(2, whole(s_q), d_q)
    normalise(1)
    mod_wait(1, whole(s_oth), d_oth)
    oth = fold_halves(d_oth[0] + d_oth[1] + d_oth[2] + d_oth[3])
    f_oth[...] = oth
    g_oth[d] = oth
    mod_wait(2, whole(s_q), d_q)
    q = (d_q[0] + d_q[1] + d_q[2] + d_q[3]).astype(BF16).astype(F32)

    kq = dot_nt(expand_heads(q, mask), wqkv_ref[1])
    for p in range(N_MOD):
        s_kq[p] = kq[p * 16 : (p + 1) * 16]
    d_kq[m] = s_kq[m]
    mod_start(3, part(s_kq), d_kq)
    dp_start(0, whole(f_oth), g_oth)
    normalise(2)
    mod_wait(3, part(s_kq), d_kq)
    kq_b = jnp.concatenate([d_kq[p] for p in range(N_MOD)], axis=1).astype(BF16)

    scores = dot_nt(kq_b, xn_ref[...]) * SCALE
    lane = lax.broadcasted_iota(jnp.int32, (16, PAD_ROWS), 1)
    image = lax.broadcasted_iota(jnp.int32, (16, PAD_ROWS), 0) >= HEADS
    valid = (((lane & 1) == 1) == image) & (lane < ROWS)
    expo = jnp.where(valid, jnp.exp(scores), 0.0)
    soft = expo / row_sum(expo)
    soft_b = soft.astype(BF16)
    w = dot(soft_b, xn_ref[...])
    for p in range(N_MOD):
        s_w[p] = w[:, p * SLICE : (p + 1) * SLICE]
    d_w[m] = s_w[m]
    mod_start(4, part(s_w), d_w)
    mod_wait(4, part(s_w), d_w)
    w64 = d_w[...].reshape(64, SLICE)

    cp = collapse_heads(dot(w64.astype(BF16), wqkv_ref[2]), mask)
    s_ctx[...] = cp
    d_ctx[m] = cp
    mod_start(5, whole(s_ctx), d_ctx)
    windows(f_ea, jnp.concatenate([w64, n0, n0], axis=0))
    g_ea[d] = f_ea[d]
    dp_start(1, part(f_ea), g_ea)
    mod_wait(5, whole(s_ctx), d_ctx)
    ctx = d_ctx[0] + d_ctx[1] + d_ctx[2] + d_ctx[3]

    ap = dot_nt(ctx.astype(BF16), wout_ref[...]) + jnp.where(t == 0, x0, 0.0)
    s_att[...] = ap
    d_att[me] = ap
    all_start(0, s_att, d_att)
    qc = jnp.concatenate([q, ctx], axis=0).astype(BF16)
    f_qc[...] = qc
    g_qc[d] = qc
    dp_start(2, whole(f_qc), g_qc)
    all_wait(0, s_att, d_att)
    hid = [d_att[p] + d_att[p + N_MOD] for p in range(N_MOD)]
    hmu = sum(row_sum(h) for h in hid) * (1.0 / D)
    hvar = sum(row_sum((h - hmu) * (h - hmu)) for h in hid) * (1.0 / D)
    hinv = lax.rsqrt(hvar + EPSILON)
    hn = (d_att[m] + d_att[m + N_MOD] - hmu) * hinv

    pp = dot(hn.astype(BF16), wproj_ref[...])
    s_prj[...] = pp
    d_prj[m] = pp
    mod_start(6, whole(s_prj), d_prj)
    hs = dot(
        jnp.concatenate([split_high_low(hn), jnp.ones((16, SLICE), BF16)], axis=0), wout_ref[...]
    )
    hs = jnp.concatenate([hs[0:8] + hs[8:16], hs[16:24]], axis=0)
    s_hs[...] = hs
    d_hs[m] = hs
    mod_start(7, whole(s_hs), d_hs)
    dp_wait(0, whole(f_oth), g_oth)
    other_f = unfold_halves(g_oth[...])
    other_inv = lax.rsqrt(row_sum(other_f * other_f) + EPSILON)
    unit = other_f * other_inv
    unit_ref[...] = unit
    unit_b = unit.astype(BF16)
    mod_wait(6, whole(s_prj), d_prj)
    proj = d_prj[0] + d_prj[1] + d_prj[2] + d_prj[3]
    pinv = lax.rsqrt(row_sum(proj * proj) + EPSILON)
    embed = proj * pinv
    emb = fold_halves(embed)
    f_emb[...] = emb
    g_emb[d] = emb
    dp_start(3, whole(f_emb), g_emb)

    def spread(k, carry):
        v = g_qc[k].astype(F32)
        qbd_ref[pl.ds(k * 64, 64), :] = expand_heads(v[0:8], mask)
        return carry

    dp_wait(2, whole(f_qc), g_qc)
    lax.fori_loop(0, N_DP, spread, 0)
    dp_wait(3, whole(f_emb), g_emb)

    emb_b = unfold_halves(g_emb[...]).astype(BF16)
    logits = dot_nt(emb_b, unit_b) * LOGIT_SCALE
    left = lax.broadcasted_iota(jnp.int32, (ALL, ALL), 0)
    right = lax.broadcasted_iota(jnp.int32, (ALL, ALL), 1)
    paired = ((left >> 1) & 3) == ((right >> 1) & 3)
    ex = jnp.where(paired, jnp.exp(logits), 0.0)
    row_total = row_sum(ex)
    col_total = jnp.sum(ex, axis=0, keepdims=True)
    grad = (0.5 / PAIRS) * (ex / row_total + ex / col_total)
    grad = grad - jnp.where(left == right, 1.0 / PAIRS, 0.0)
    grad_ref[...] = grad
    grad8 = grad_ref[pl.ds(d * GROUP, GROUP), :].astype(BF16)
    d_embed = LOGIT_SCALE * dot(grad8, unit_b)
    d_proj = (d_embed - embed * row_sum(embed * d_embed)) * pinv
    d_proj_b = d_proj.astype(BF16)
    dh = dot_nt(d_proj_b, wproj_ref[...])
    da = dot(split_high_low(dh), wout_ref[...])
    lane = lax.broadcasted_iota(jnp.int32, (GROUP, 128), 1)
    stats = jnp.where(lane == 0, row_sum(dh), jnp.where(lane == 1, row_sum(dh * hn), 0.0))
    da = jnp.concatenate([da[0:8] + da[8:16], stats], axis=1)
    s_dh[...] = da
    d_dh[m] = da
    mod_start(8, whole(s_dh), d_dh)
    dpr = fold_halves(d_proj)
    f_dpr[...] = dpr
    g_dpr[d] = dpr
    dp_start(4, whole(f_dpr), g_dpr)

    rows_m = ((lax.broadcasted_iota(jnp.int32, (ALL, 1), 0) >> 1) & 3) == m
    cols_m = ((lax.broadcasted_iota(jnp.int32, (1, ALL), 1) >> 1) & 3) == m
    diag = row_sum(jnp.where(left == right, logits, 0.0))
    loss = jnp.sum(
        jnp.where(rows_m, 0.5 * jnp.log(row_total) - diag, 0.0), axis=0, keepdims=True
    ) + row_sum(jnp.where(cols_m, 0.5 * jnp.log(col_total), 0.0))
    loss_ref[...] = jnp.broadcast_to(loss * (1.0 / PAIRS), (8, 128))
    d_unit = LOGIT_SCALE * dot_tn(grad.astype(BF16), emb_b)
    grad_other = (d_unit - unit * row_sum(unit * d_unit)) * other_inv
    unit_ref[...] = grad_other
    gother_ref[...] = own_rows(unit_ref[pl.ds(d * GROUP, GROUP), :])

    mod_wait(7, whole(s_hs), d_hs)
    hs = d_hs[0] + d_hs[1] + d_hs[2] + d_hs[3]
    mod_wait(8, whole(s_dh), d_dh)
    da = d_dh[0] + d_dh[1] + d_dh[2] + d_dh[3]
    m1 = da[:, HALF : HALF + 1] * (1.0 / D)
    m2 = da[:, HALF + 1 : HALF + 2] * (1.0 / D)
    d_context = hinv * (da[:, :HALF] - m1 * hs[8:16] - m2 * hs[0:8])
    d_hidden = hinv * (dh - m1 - hn * m2)

    vd = dot_nt(expand_heads(d_context, mask), wqkv_ref[2])
    for p in range(N_MOD):
        s_vd[p] = jnp.concatenate([vd[p * 16 : (p + 1) * 16], d_hidden], axis=0)
    d_vd[m] = s_vd[m]
    mod_start(9, part(s_vd), d_vd)
    mod_wait(9, part(s_vd), d_vd)
    vd_b = jnp.concatenate([d_vd[p, 0:16] for p in range(N_MOD)], axis=1).astype(BF16)
    d_soft = dot_nt(vd_b, xn_ref[...])
    d_score = soft * (d_soft - row_sum(soft * d_soft))
    d_score_b = d_score.astype(BF16)
    u = dot(d_score_b, xn_ref[...]) * SCALE
    for p in range(N_MOD):
        s_u[p] = u[:, p * SLICE : (p + 1) * SLICE]
    d_u[m] = s_u[m]
    mod_start(10, part(s_u), d_u)
    s_sc[0:16] = (d_score * SCALE).astype(BF16)
    s_sc[16:32] = soft_b
    s_kv[0:16] = kq_b
    s_kv[16:32] = vd_b
    tp_copy(0, s_sc, d_sc).start()
    tp_copy(1, s_kv, d_kv).start()
    mod_wait(10, part(s_u), d_u)
    u64 = d_u[...].reshape(64, SLICE)
    dqp = collapse_heads(dot(u64.astype(BF16), wqkv_ref[1]), mask)
    s_dq[...] = dqp
    d_dq[m] = dqp
    mod_start(11, whole(s_dq), d_dq)
    windows(f_la, jnp.concatenate([u64, hn, d_hidden], axis=0))
    g_la[d] = f_la[d]
    dp_start(5, part(f_la), g_la)
    mod_wait(11, whole(s_dq), d_dq)
    dq = d_dq[0] + d_dq[1] + d_dq[2] + d_dq[3]
    dd = jnp.concatenate([dq, d_context], axis=0).astype(BF16)
    f_dd[...] = dd
    g_dd[d] = dd
    dp_start(6, whole(f_dd), g_dd)
    cg = dot_nt(dq.astype(BF16), wqkv_ref[0])
    s_cg[...] = cg
    d_cg[me] = cg
    all_start(1, s_cg, d_cg)

    tp_copy(0, s_sc, d_sc).wait_recv()
    tp_copy(1, s_kv, d_kv).wait_recv()
    weights = jnp.concatenate([s_sc[...], d_sc[...]], axis=0).astype(F32).T.astype(BF16)
    factors = jnp.concatenate([s_kv[...], d_kv[...]], axis=0)
    half = pl.ds(pl.multiple_of(t * HALF, 128), HALF)
    for c in range(PAD_ROWS // CHUNK):
        at = pl.ds(c * CHUNK, CHUNK)
        dn = dot(weights[c * CHUNK : (c + 1) * CHUNK], factors)
        mu, inv = mu_ref[at, :], inv_ref[at, :]
        xh = (x_ref[at, :].astype(F32) - mu) * inv
        mean_grad = row_sum(dn) * (1.0 / D)
        mean_cross = row_sum(dn * xh) * (1.0 / D)
        dn_ref[...] = dn
        if c == 0:
            dn0_ref[...] = dn[0:8]
        xh = (x_ref[at, half].astype(F32) - mu) * inv
        gtok_ref[at, :] = (inv * (dn_ref[:, half] - mean_grad - xh * mean_cross)).astype(BF16)

    all_wait(1, s_cg, d_cg)
    extra = own_rows(
        jnp.concatenate([d_cg[p] + d_cg[p + N_MOD] for p in range(N_MOD)], axis=1)
    )
    dn = dn0_ref[...] + extra
    mu, inv = mu_ref[0:8, :], inv_ref[0:8, :]
    xh = (x_ref[0:16, :].astype(F32)[0:8] - mu) * inv
    mean_grad = row_sum(dn) * (1.0 / D)
    mean_cross = row_sum(dn * xh) * (1.0 / D)
    dn0_ref[...] = inv * (dn - mean_grad - xh * mean_cross) + own_rows(
        jnp.concatenate([d_vd[p, 16:24] for p in range(N_MOD)], axis=1)
    )
    head_rows = gtok_ref[0:16, :].astype(F32)
    head_rows = jnp.concatenate(
        [jnp.where(row8 < 2, dn0_ref[:, half], head_rows[0:8]), head_rows[8:16]], axis=0
    )
    gtok_ref[0:16, :] = head_rows.astype(BF16)

    dp_wait(1, part(f_ea), g_ea)
    dp_wait(4, whole(f_dpr), g_dpr)
    dp_wait(5, part(f_la), g_la)
    la = g_la[...]
    gk = dot_tn(la[:, 0:64].reshape(1024, 128), qbd_ref[...])
    gqkv_ref[1] = gk[0:OUT_ROWS]
    tail = la[:, 64:80].astype(F32)
    hn_all = tail[:, 0:8].reshape(ALL, 128).astype(BF16)
    dhid_all = tail[:, 8:16].reshape(ALL, 128).astype(BF16)
    gproj_ref[...] = dot_tn(hn_all, unfold_halves(g_dpr[...]).astype(BF16))[0:OUT_ROWS]
    ctx_all = g_qc[...].astype(F32)[:, 8:16].reshape(ALL, HALF).astype(BF16)
    gout_ref[...] = dot_tn(dhid_all, ctx_all)[0:OUT_ROWS]
    dp_wait(6, whole(f_dd), g_dd)

    def spread_late(k, carry):
        v = g_dd[k].astype(F32)
        dbd_ref[pl.ds(k * 64, 64), :] = expand_heads(v[8:16], mask)
        return carry

    lax.fori_loop(0, N_DP, spread_late, 0)
    ea = g_ea[...]
    gv = dot_tn(ea[:, 0:64].reshape(1024, 128), dbd_ref[...])
    gqkv_ref[2] = gv[0:OUT_ROWS]
    n0_all = ea[:, 64:80].astype(F32)[:, 0:8].reshape(ALL, 128).astype(BF16)
    dq_all = g_dd[...].astype(F32)[:, 0:8].reshape(ALL, HALF).astype(BF16)
    gqkv_ref[0] = dot_tn(n0_all, dq_all)[0:OUT_ROWS]

    for n, src, dst in (
        (0, part(s_cls), d_cls), (1, whole(s_oth), d_oth), (2, whole(s_q), d_q),
        (3, part(s_kq), d_kq), (4, part(s_w), d_w), (5, whole(s_ctx), d_ctx),
        (6, whole(s_prj), d_prj), (7, whole(s_hs), d_hs), (8, whole(s_dh), d_dh),
        (9, part(s_vd), d_vd), (10, part(s_u), d_u), (11, whole(s_dq), d_dq),
    ):
        mod_end(n, src, dst)
    all_end(0, s_att, d_att)
    all_end(1, s_cg, d_cg)
    tp_copy(0, s_sc, d_sc).wait_send()
    tp_copy(1, s_kv, d_kv).wait_send()
    for n, src, dst in (
        (0, whole(f_oth), g_oth), (1, part(f_ea), g_ea), (2, whole(f_qc), g_qc),
        (3, whole(f_emb), g_emb), (4, whole(f_dpr), g_dpr), (5, part(f_la), g_la),
        (6, whole(f_dd), g_dd),
    ):
        dp_end(n, src, dst)


def local(tokens, w_qkv, w_out, w_proj, other_emb):
    rows = tokens.transpose(1, 0, 2).reshape(ROWS, D)
    rows = jnp.pad(rows, ((0, PAD_ROWS - ROWS), (0, 0)))
    vmem = pl.BlockSpec(memory_space=pltpu.VMEM)

    def pair(send, land, dtype=F32):
        return [pltpu.VMEM(send, dtype), pltpu.VMEM(land, dtype)]

    def mod_all(n, k):
        return pair((n, k), (N_MOD, n, k))

    def mod_each(n):
        return pair((N_MOD, n, SLICE), (N_MOD, n, SLICE))

    def dp_all(n, k):
        return pair((n, k), (N_DP, n, k), BF16)

    scratch = [
        pltpu.VMEM((PAD_ROWS, D), BF16),
        pltpu.VMEM((PAD_ROWS, 1), F32),
        pltpu.VMEM((PAD_ROWS, 1), F32),
        pltpu.VMEM((ALL, ALL), F32),
        pltpu.VMEM((CHUNK, D), F32),
        pltpu.VMEM((8, D), F32),
        pltpu.VMEM((ALL, E), F32),
        pltpu.VMEM((N_DP * 64, HALF), BF16),
        pltpu.VMEM((N_DP * 64, HALF), BF16),
    ]
    scratch += mod_each(16) + mod_all(8, E) + mod_all(8, HALF) + mod_each(16) + mod_each(16)
    scratch += mod_all(8, HALF) + pair((8, SLICE), (2 * N_MOD, 8, SLICE)) + mod_all(8, E)
    scratch += mod_all(16, HALF) + mod_all(8, HALF + 128) + mod_each(24) + mod_each(16)
    scratch += mod_all(8, HALF) + pair((8, SLICE), (2 * N_MOD, 8, SLICE))
    scratch += pair((32, PAD_ROWS), (32, PAD_ROWS), BF16) + pair((32, D), (32, D), BF16)
    scratch += dp_all(16, E // 2) + dp_all(16, E // 2) + dp_all(16, E // 2) + dp_all(16, HALF)
    scratch += dp_all(16, HALF) + pair((N_DP, 80, 128), (N_DP, 80, 128), BF16) * 2
    dma = pltpu.SemaphoreType.DMA
    scratch += [dma((12, N_MOD)), dma((12, N_MOD)), dma((2, 8)), dma((2, 8)), dma((2,)), dma((2,))]
    scratch += [dma((7, N_DP)), dma((7, N_DP))]
    loss, grad_rows, grad_qkv, grad_out, grad_proj, grad_other = pl.pallas_call(
        kernel,
        out_shape=[
            jax.ShapeDtypeStruct((8, 128), F32),
            jax.ShapeDtypeStruct((PAD_ROWS, HALF), BF16),
            jax.ShapeDtypeStruct((3, OUT_ROWS, HALF), F32),
            jax.ShapeDtypeStruct((OUT_ROWS, HALF), F32),
            jax.ShapeDtypeStruct((OUT_ROWS, E), F32),
            jax.ShapeDtypeStruct((8, E), F32),
        ],
        in_specs=[vmem] * 5,
        out_specs=[vmem] * 6,
        scratch_shapes=scratch,
        compiler_params=pltpu.CompilerParams(
            collective_id=0, has_side_effects=True, vmem_limit_bytes=48 * 2**20
        ),
    )(rows, w_qkv.transpose(1, 0, 2), w_out, w_proj, other_emb)
    grad_tokens = grad_rows[:ROWS].reshape(TOK, IMGS, HALF).transpose(1, 0, 2)
    return (
        loss[0, 0:1],
        grad_tokens,
        grad_qkv.transpose(1, 0, 2),
        grad_out,
        grad_proj,
        grad_other[0:IMGS].astype(BF16),
    )


def solution(mesh):
    placed = (
        P(("mod", "dp"), None, None),
        P("mod", None, "tp"),
        P("mod", "tp"),
        P("mod", None),
        P(("mod", "dp"), None),
    )
    return jax.shard_map(
        local,
        mesh=mesh,
        in_specs=placed,
        out_specs=(
            P("mod"),
            P(("mod", "dp"), None, "tp"),
            P(("mod", "dp"), None, "tp"),
            P(("mod", "dp"), "tp"),
            P(("mod", "dp"), None),
            P(("mod", "dp"), None),
        ),
        check_vma=False,
    )
```

time: 1010 us -> 77.7 us (0.08); the launches traced: 994 us -> 77.5 us
  waiting for transfers between devices: 774 us -> 0 us
  Pallas kernels: 0 us -> 67.3 us
  blocking collectives: 63.1 us -> 0 us
  local copies, waits for them, and re-layouts: 60 us -> 9.52 us
  other arithmetic: 43.8 us -> 0 us
  matrix products: 32.6 us -> 0 us
  between operations: 19.5 us -> 0.69 us
    unnamed x8 -> x0, waiting for transfers between devices: 657 us -> none
    pallas_call x0 -> x1, Pallas kernels: none -> 67.3 us  [local(): pl.pallas_call(kernel, out_shape=[jax.ShapeDtypeStruct((8, 128), F32), ja...]
    all_gather x3 -> x0, waiting for transfers between devices: 62.3 us -> none  [the longest x1 25.9 us: local(): lax.all_gather(w_qkv, 'mod', axis=0, tiled=True)]
    psum x1 -> x0, waiting for transfers between devices: 54.7 us -> none  [local(): lax.psum(d_normed.astype(jnp.bfloat16), 'tp').astype(jnp.float32)]
    psum x2 -> x0, blocking collectives: 42.8 us -> none  [the longest x1 34 us: local(): col_total, piece_total = lax.psum((col_part, loss_piece), 'dp')]
    dot_general x15 -> x0, matrix products: 32.6 us -> none  [the longest x5 14.5 us: contract_first(): lax.dot_general(left, right, (((0,), (0,)), ((), ())), preferred_element_...]
    slice x6 -> x3, local copies, waits for them, and re-layouts: 26 us -> 1.17 us  [the longest x1 0.6 us: local(): grad_other[0:IMGS].astype(BF16)]
    all_gather x1 -> x0, blocking collectives: 20.3 us -> none  [local(): pair_all = lax.all_gather(other_b, 'dp', axis=0, tiled=True)]
  transfers between devices with their start and end apart: 6 -> 0, of which waited for: 6 -> 0; matrix products, arithmetic and copies ran while one was open for 8% -> 0% of each run, Pallas kernels for 0% -> 0%
where the time goes in v1:
time: 77.7 us; the launch traced here: 77.5 us
  Pallas kernels  67.3 us (87%)
  local copies, waits for them, and re-layouts  9.52 us (12%)
    pallas_call x1, Pallas kernels, local(): pl.pallas_call(kernel, out_shape=[jax.ShapeDtypeStruct((8, 128), F32), ja...  67.3 us
    unnamed x11, local copies, waits for them, and re-layouts  3.38 us
    reshape x1, local copies, waits for them, and re-layouts, local(): rows = tokens.transpose(1, 0, 2).reshape(ROWS, D)  3.21 us
    reshape x1, local copies, waits for them, and re-layouts, local(): grad_tokens = grad_rows[:ROWS].reshape(TOK, IMGS, HALF).transpose(1, 0, 2)  1.68 us

profile of v1, /device:TPU:1, one launch (start us, length us, event | category | flops | bytes accessed | tf_op | source)
XLA Modules:
  0.0 77.5 jit_solution(15696642553894683839)
XLA Ops:
  0.6 3.2 %reshape.18 = bf16[514,1280]{1,0:T(8,128)(2,1)S(1)} reshape(bf16[257,2,1280]{2,1,0:T(2,128)(2,1)} %bitcast.7) | data formatting | bytes 2631680 | tf_op jit(solution)/shard_map/reshape | solution.py:531
  3.8 0.0 copy-start
  3.9 0.0 copy-start.1
  3.9 0.0 copy-start.2
  3.9 0.0 copy-start.3
  3.9 0.1 pad.4.x_ref
  4.0 1.1 %copy-done = bf16[320,3,640]{2,0,1:T(8,128)(2,1)S(1)} copy-done((bf16[320,3,640]{2,0,1:T(8,128)(2,1)S(1)}, bf16[320,3,640]{2,0,1:T(8,128)(2,1)}, u32[]{:S(2)}) %copy-start) | copy-done | bytes 1228824
  5.1 0.2 copy-done.1
  5.3 0.1 copy-done.2
  5.4 0.0 copy-done.3
  5.4 67.3 %shard_map.100 = (f32[8,128]{1,0:T(8,128)S(1)}, bf16[528,640]{1,0:T(8,128)(2,1)S(1)}, f32[3,20,640]{2,1,0:T(8,128)S(1)}, f32[20,640]{1,0:T(8,128)S(1)}, f32[20,1024]{1,0:T(8,128)S(1)}, /*index=5*/f32[8,1024]{1,0:T(8,128)S(1)}) custom-call(bf16[528,1280]{1,0:T(8,128)(2,1)S(1)} %pad.4.x_ref, bf16[3,320,640]{2,1,0:T(8,128)(2,1)S(1)} %bitcast.5, ...), custom_call_target="tpu_custom_call" | custom-call | tf_op jit(solution)/shard_map/pallas_call | solution.py:568
  72.7 0.5 slice.10
  73.3 0.6 slice.15
  73.9 0.1 slice.11
  73.9 1.7 %reshape.19 = bf16[257,2,640]{2,1,0:T(2,128)(2,1)} reshape(bf16[514,640]{1,0:T(8,128)(2,1)S(1)} %slice.11) | data formatting | bytes 1315840 | tf_op jit(solution)/shard_map/reshape | solution.py:585
  75.6 0.7 copy.14
  76.3 0.6 copy.15
  76.9 0.6 copy.16
Async XLA Ops:
  3.8 1.3 %copy-start = (bf16[320,3,640]{2,0,1:T(8,128)(2,1)S(1)}, bf16[320,3,640]{2,0,1:T(8,128)(2,1)}, u32[]{:S(2)}) copy-start(bf16[320,3,640]{2,0,1:T(8,128)(2,1)} %param.6) | copy-start | bytes 3686404
  3.9 1.4 %copy-start.1 = (bf16[320,1024]{1,0:T(8,128)(2,1)S(1)}, bf16[320,1024]{1,0:T(8,128)(2,1)}, u32[]{:S(2)}) copy-start(bf16[320,1024]{1,0:T(8,128)(2,1)} %wproj_ref.1) | copy-start | bytes 1966084
  3.9 1.5 %copy-start.2 = (bf16[320,640]{1,0:T(8,128)(2,1)S(1)}, bf16[320,640]{1,0:T(8,128)(2,1)}, u32[]{:S(2)}) copy-start(bf16[320,640]{1,0:T(8,128)(2,1)} %wout_ref.1) | copy-start | bytes 1228804
  3.9 1.5 %copy-start.3 = (bf16[2,1024]{1,0:T(2,128)(2,1)S(1)}, bf16[2,1024]{1,0:T(2,128)(2,1)}, u32[]{:S(2)}) copy-start(bf16[2,1024]{1,0:T(2,128)(2,1)} %other_ref.1) | copy-start | bytes 12292

commit v2 on v1

v2 whole, which is shorter than its diff:
```python
import functools

import jax
import jax.numpy as jnp
from jax import lax
from jax.experimental import pallas as pl
from jax.experimental.pallas import tpu as pltpu
from jax.sharding import PartitionSpec as P

HEAD_DIM = 80
EPSILON = 1e-06
LOGIT_SCALE = 1.0 / 0.07
MESH = pl.DeviceIdType.MESH
F32 = jnp.float32
BF16 = jnp.bfloat16

N_MOD, N_DP, N_TP = 4, 16, 2
IMGS = 2
GROUP = N_MOD * IMGS
HEADS = 8
TOK = 257
ROWS = IMGS * TOK
PAD_ROWS = 528
PAD_TOK = PAD_ROWS // IMGS
CHUNK = 176
D = 1280
HALF = D // 2
SLICE = D // N_MOD
OUT_ROWS = SLICE // N_DP
E = 1024
PAIRS = 32
ALL = GROUP * N_DP
SCALE = HEAD_DIM**-0.5
COLUMNS = (512, 512, 640, 640, 640)
ROWS_BY_X = (True, False, False, True, True)
PIECE = SLICE // 4


def dot(a, b):
    return jnp.dot(a, b, preferred_element_type=F32)


def dot_nt(a, b):
    return lax.dot_general(a, b, (((1,), (1,)), ((), ())), preferred_element_type=F32)


def dot_tn(a, b):
    return lax.dot_general(a, b, (((0,), (0,)), ((), ())), preferred_element_type=F32)


def blocks(v):
    return jnp.concatenate(
        [v[:, k : k + 128] for k in range(0, v.shape[1], 128)], axis=0
    )


def unblocks(v):
    n = v.shape[0] * 8
    return jnp.concatenate(
        [v[:, k : k + 8].reshape(n, 128) for k in range(0, v.shape[1], 8)], axis=1
    )


def head_mask():
    lane = lax.broadcasted_iota(jnp.int32, (HEADS, HALF), 1)
    head = lax.broadcasted_iota(jnp.int32, (HEADS, HALF), 0) * HEAD_DIM
    return (lane >= head) & (lane < head + HEAD_DIM)


def expand_heads(v, mask):
    return jnp.concatenate(
        [jnp.where(mask, v[b : b + 1], 0.0) for b in range(GROUP)], axis=0
    ).astype(BF16)


def collapse_heads(v, mask):
    return jnp.concatenate(
        [
            jnp.sum(
                jnp.where(mask, v[b * HEADS : (b + 1) * HEADS], 0.0), axis=0, keepdims=True
            )
            for b in range(GROUP)
        ],
        axis=0,
    )


def row_sum(v):
    return jnp.sum(v, axis=-1, keepdims=True)


def kernel(
    x_hbm, wqkv_hbm, wout_hbm, wproj_hbm, other_hbm,
    loss_ref, gtok_ref, gqkv_ref, gout_ref, gproj_ref, gother_ref,
    other_ref, pairs_ref, x_ref, wq_ref, wp0_ref, wp1_ref, wo_ref, wv_ref, wk_ref,
    xn_ref, mu_ref, inv_ref, grad_ref, dn_ref, dn0_ref, unit_ref, qbd_ref, dbd_ref, hn_ref, dhid_ref,
    s_cls, d_cls, s_oth, d_oth, s_q, d_q, s_kq, d_kq, s_w, d_w, s_ctx, d_ctx, s_att, d_att,
    s_u, d_u, s_cg, d_cg, s_sc, d_sc, s_kv, d_kv,
    f_oth, g_oth, f_emb, g_emb, f_a, g_a, f_b, g_b, f_c, g_c,
    load_sem, y_send, y_recv, b_send, b_recv, a_send, a_recv, core_send, core_recv,
    mod_send, mod_recv, all_send, all_recv, tp_send, tp_recv, dp_send, dp_recv,
):
    m, d, t = lax.axis_index("mod"), lax.axis_index("dp"), lax.axis_index("tp")
    me = t * N_MOD + m
    cx, cz = d // 4, lax.rem(d, 4)
    across = lax.rem(m + 2, N_MOD)
    sibling = m + 1 - 2 * lax.rem(m, 2)

    barrier = pltpu.get_barrier_semaphore()
    for k in range(1, N_MOD):
        pl.semaphore_signal(
            barrier, 1, device_id=(lax.rem(m + k, N_MOD), d, t), device_id_type=MESH
        )
    for k in range(N_MOD):
        pl.semaphore_signal(
            barrier, 1, device_id=(lax.rem(m + k, N_MOD), d, 1 - t), device_id_type=MESH
        )

    def greet(k, carry):
        pl.semaphore_signal(
            barrier, 1, device_id=(m, lax.rem(d + k, N_DP), t), device_id_type=MESH
        )
        return carry

    lax.fori_loop(1, N_DP, greet, 0)

    sources = (
        wproj_hbm.at[:, pl.ds(0, 512)], wproj_hbm.at[:, pl.ds(512, 512)], wout_hbm,
        wqkv_hbm.at[2], wqkv_hbm.at[1],
    )
    gathered = (wp0_ref, wp1_ref, wo_ref, wv_ref, wk_ref)
    load_x = pltpu.make_async_copy(x_hbm, pairs_ref, load_sem.at[6])
    load_x.start()
    load_other = pltpu.make_async_copy(other_hbm, other_ref, load_sem.at[7])
    load_other.start()
    load_q = pltpu.make_async_copy(wqkv_hbm.at[0], wq_ref, load_sem.at[5])
    load_q.start()
    loads = [
        pltpu.make_async_copy(src, dst.at[m], load_sem.at[i])
        for i, (src, dst) in enumerate(zip(sources, gathered))
    ]
    for i in (4, 3, 2, 0, 1):
        loads[i].start()

    leaving = []

    def remote(src, dst, send, recv, peer):
        return pltpu.make_async_remote_copy(
            src, dst, send, recv, device_id=peer, device_id_type=MESH
        )

    def start(copy):
        copy.start()

    def go(copy):
        copy.start()
        leaving.append(copy.wait_send)

    def rows_of(i, step):
        c = cx if ROWS_BY_X[i] else cz
        return pl.ds(pl.multiple_of(lax.rem(c + step, 4) * PIECE, 16), PIECE)

    def cols_of(i, step):
        c = cz if ROWS_BY_X[i] else cx
        return pl.ds(pl.multiple_of(lax.rem(c + step, 4) * 128, 128), 128)

    def row_peer(i, step):
        along_x = (m, lax.rem(cx + step, 4) * 4 + cz, t)
        along_z = (m, cx * 4 + lax.rem(cz + step, 4), t)
        return along_x if ROWS_BY_X[i] else along_z

    def col_peer(i, step):
        along_x = (m, lax.rem(cx + step, 4) * 4 + cz, t)
        along_z = (m, cx * 4 + lax.rem(cz + step, 4), t)
        return along_z if ROWS_BY_X[i] else along_x

    def pieces(i):
        yield 0, cols_of(i, 0)
        if COLUMNS[i] == 640:
            yield 1, pl.ds(512, 128)

    def fetch_core(i):
        go(remote(
            sources[i], gathered[i].at[m], core_send.at[i, 0], core_recv.at[i, 0], (sibling, d, t)
        ))

    def fetch_across(i):
        for n, cols in pieces(i):
            go(remote(
                sources[i].at[rows_of(i, 0), cols], gathered[i].at[m, rows_of(i, 0), cols],
                y_send.at[i, n], y_recv.at[i, n], (across, d, t),
            ))

    def share_cols(i):
        for n, cols in pieces(i):
            part_ref = gathered[i].at[across, rows_of(i, 0), cols]
            remote(
                part_ref, part_ref, y_send.at[i, n], y_recv.at[i, n], (across, d, t)
            ).wait_recv()
        part_ref = gathered[i].at[across, rows_of(i, 0), cols_of(i, 0)]
        for k in (2, 1, 3):
            start(remote(part_ref, part_ref, b_send.at[i], b_recv.at[i], col_peer(i, k)))
        three = gathered[i].at[across, pl.ds(0, PIECE), pl.ds(0, 384)]
        leaving.append(
            remote(three, three, b_send.at[i], b_recv.at[i], col_peer(i, 1)).wait_send
        )

    def share_rows(i):
        three = gathered[i].at[across, pl.ds(0, PIECE), pl.ds(0, 384)]
        remote(three, three, b_send.at[i], b_recv.at[i], col_peer(i, 1)).wait_recv()
        part_ref = gathered[i].at[across, rows_of(i, 0)]
        for k in (2, 1, 3):
            start(remote(part_ref, part_ref, a_send.at[i], a_recv.at[i], row_peer(i, k)))
        three = gathered[i].at[across, pl.ds(0, 3 * PIECE)]
        leaving.append(
            remote(three, three, a_send.at[i], a_recv.at[i], row_peer(i, 1)).wait_send
        )

    def share_core(i):
        three = gathered[i].at[across, pl.ds(0, 3 * PIECE)]
        remote(three, three, a_send.at[i], a_recv.at[i], row_peer(i, 1)).wait_recv()
        block = gathered[i].at[across]
        go(remote(block, block, core_send.at[i, 1], core_recv.at[i, 1], (sibling, d, t)))

    def complete(i):
        for n, owner in ((0, sibling), (1, lax.rem(sibling + 2, N_MOD))):
            block = gathered[i].at[owner]
            remote(
                block, block, core_send.at[i, n], core_recv.at[i, n], (sibling, d, t)
            ).wait_recv()

    def arrivals(dst, count, send, recv, peer):
        ref = dst.at[pl.ds(0, count)]
        return remote(ref, ref, send, recv, peer)

    def mod_all(n, dst):
        return arrivals(dst, N_MOD - 1, mod_send.at[n], mod_recv.at[n], (sibling, d, t))

    def mod_start(n, src, dst):
        for k in (2, 1, 3):
            peer = lax.rem(m + k, N_MOD)
            start(remote(src(peer), dst.at[m], mod_send.at[n], mod_recv.at[n], (peer, d, t)))
        leaving.append(lambda: mod_all(n, dst).wait_send())

    def mod_wait(n, dst):
        mod_all(n, dst).wait_recv()

    def all_all(n, dst):
        return arrivals(dst, 2 * N_MOD - 1, all_send.at[n], all_recv.at[n], (sibling, d, t))

    def all_start(n, src, dst):
        for k in range(2 * N_MOD - 1, 0, -1):
            peer = (lax.rem(m + k, N_MOD), d, t if k < N_MOD else 1 - t)
            start(remote(src, dst.at[me], all_send.at[n], all_recv.at[n], peer))
        leaving.append(lambda: all_all(n, dst).wait_send())

    def all_wait(n, dst):
        all_all(n, dst).wait_recv()

    def dp_all(n, dst):
        return arrivals(
            dst, N_DP - 1, dp_send.at[n], dp_recv.at[n], (m, lax.rem(d + 1, N_DP), t)
        )

    def dp_start(n, src, dst):
        def body(k, carry):
            peer = lax.rem(d + k, N_DP)
            start(remote(src(peer), dst.at[d], dp_send.at[n], dp_recv.at[n], (m, peer, t)))
            return carry

        lax.fori_loop(1, N_DP, body, 0)
        leaving.append(lambda: dp_all(n, dst).wait_send())

    def dp_wait(n, dst):
        dp_all(n, dst).wait_recv()

    def tp_copy(n, src, dst):
        return remote(src, dst, tp_send.at[n], tp_recv.at[n], (m, d, 1 - t))

    def whole(ref):
        return lambda peer: ref

    def part(ref):
        return lambda peer: ref.at[peer]

    row8 = lax.broadcasted_iota(jnp.int32, (GROUP, 1), 0)
    mask = head_mask()

    def place(v):
        return jnp.where(row8 == 2 * m, v[0:1], jnp.where(row8 == 2 * m + 1, v[1:2], 0.0))

    def own_rows(v):
        first = jnp.sum(jnp.where(row8 == 2 * m, v, 0.0), axis=0, keepdims=True)
        second = jnp.sum(jnp.where(row8 == 2 * m + 1, v, 0.0), axis=0, keepdims=True)
        return jnp.where(row8 == 0, first, jnp.where(row8 == 1, second, 0.0))

    def normalise(c):
        at = pl.ds(c * CHUNK, CHUNK)
        x = x_ref[at, :].astype(F32)
        mu = row_sum(x) * (1.0 / D)
        x = x - mu
        inv = lax.rsqrt(row_sum(x * x) * (1.0 / D) + EPSILON)
        xn_ref[at, :] = (x * inv).astype(BF16)
        mu_ref[at, :] = mu
        inv_ref[at, :] = inv

    def window(v, k):
        wide = jnp.concatenate([v, jnp.zeros((v.shape[0], 192), F32)], axis=1)
        return wide[:, k * OUT_ROWS : k * OUT_ROWS + 128]

    def folded(v, k):
        wide = jnp.concatenate([v, jnp.zeros((64, 64), F32)], axis=1)
        at = k * OUT_ROWS
        return jnp.concatenate([wide[0:32, at : at + 64], wide[32:64, at : at + 64]], axis=1)

    def spread(dst, k, v):
        v = expand_heads(v, mask)
        at = pl.ds(pl.multiple_of(k * 32, 32), 32)
        dst[0, at, :] = v[0:32]
        dst[1, at, :] = v[32:64]

    def head_grad(factor, dst):
        factor = factor.reshape(N_DP * 32, 128)
        return dot_tn(factor, dst[0])[0:OUT_ROWS] + dot_tn(factor, dst[1])[64 : 64 + OUT_ROWS]

    def columns(v):
        return [v[:, p * SLICE : (p + 1) * SLICE] for p in range(N_MOD)]

    def full(ref):
        return ref[...].reshape(D, ref.shape[2])

    load_other.wait()
    load_x.wait()
    x8 = pairs_ref[0].astype(F32)
    mu8 = row_sum(x8) * (1.0 / D)
    c8 = x8 - mu8
    n8 = c8 * lax.rsqrt(row_sum(c8 * c8) * (1.0 / D) + EPSILON)
    for p, v in enumerate(columns(jnp.concatenate([place(n8), place(x8)], axis=0))):
        s_cls[p] = v
    d_cls[m] = s_cls[m]
    oth = place(other_ref[...].astype(F32))
    s_oth[...] = oth
    d_oth[m] = oth
    pl.semaphore_wait(barrier, N_MOD - 1 + N_MOD + N_DP - 1)
    mod_start(0, part(s_cls), d_cls)
    for i in (0, 1):
        fetch_across(i)
    for i in (0, 1):
        fetch_core(i)

    def interleave(k, carry):
        rows = pairs_ref[pl.ds(k * 16, 16)].astype(F32).reshape(32, D)
        x_ref[pl.ds(pl.multiple_of(k * 32, 32), 32), :] = rows.astype(BF16)
        return carry

    lax.fori_loop(0, 16, interleave, 0)
    last = jnp.concatenate([pairs_ref[TOK - 1].astype(F32), jnp.zeros((14, D), F32)], axis=0)
    x_ref[512:PAD_ROWS, :] = last.astype(BF16)
    normalise(0)
    load_q.wait()
    mod_wait(0, d_cls)
    cls = d_cls[0] + d_cls[1] + d_cls[2] + d_cls[3]
    n0, x0 = cls[0:8], cls[8:16]

    qp = dot(n0.astype(BF16), wq_ref[...])
    s_q[...] = qp
    d_q[m] = qp
    mod_start(1, whole(s_q), d_q)
    for i in (2, 3, 4):
        fetch_across(i)
    mod_start(2, whole(s_oth), d_oth)
    normalise(1)
    for i in (0, 1):
        share_cols(i)
    loads[4].wait()
    mod_wait(1, d_q)
    q = (d_q[0] + d_q[1] + d_q[2] + d_q[3]).astype(BF16).astype(F32)

    kq = dot_nt(expand_heads(q, mask), wk_ref[m])
    for p in range(N_MOD):
        s_kq[p] = kq[p * 16 : (p + 1) * 16]
    d_kq[m] = s_kq[m]
    mod_start(3, part(s_kq), d_kq)
    for i in (2, 3, 4):
        fetch_core(i)
    normalise(2)
    for i in (2, 3, 4):
        share_cols(i)
    for i in (0, 1):
        share_rows(i)
    mod_wait(3, d_kq)
    kq_b = jnp.concatenate([d_kq[p] for p in range(N_MOD)], axis=1).astype(BF16)

    scores = dot_nt(kq_b, xn_ref[...]) * SCALE
    lane = lax.broadcasted_iota(jnp.int32, (16, PAD_ROWS), 1)
    image = lax.broadcasted_iota(jnp.int32, (16, PAD_ROWS), 0) >= HEADS
    valid = (((lane & 1) == 1) == image) & (lane < ROWS)
    expo = jnp.where(valid, jnp.exp(scores), 0.0)
    soft = expo / row_sum(expo)
    soft_b = soft.astype(BF16)
    w = dot(soft_b, xn_ref[...])
    for p, v in enumerate(columns(w)):
        s_w[p] = v
    d_w[m] = s_w[m]
    mod_start(4, part(s_w), d_w)
    for i in (2, 3, 4):
        share_rows(i)
    mod_wait(2, d_oth)
    oth = blocks(d_oth[0] + d_oth[1] + d_oth[2] + d_oth[3]).astype(BF16)
    f_oth[...] = oth
    g_oth[d] = oth
    dp_start(0, whole(f_oth), g_oth)
    loads[3].wait()
    mod_wait(4, d_w)
    w64 = d_w[...].reshape(64, SLICE)

    cp = collapse_heads(dot(w64.astype(BF16), wv_ref[m]), mask)
    s_ctx[...] = cp
    d_ctx[m] = cp
    mod_start(5, whole(s_ctx), d_ctx)
    loads[2].wait()
    mod_wait(5, d_ctx)
    ctx = d_ctx[0] + d_ctx[1] + d_ctx[2] + d_ctx[3]

    ap = dot_nt(ctx.astype(BF16), wo_ref[m]) + jnp.where(t == 0, x0, 0.0)
    s_att[...] = ap
    d_att[me] = ap
    all_start(0, s_att, d_att)
    common = jnp.concatenate([blocks(q), blocks(ctx), jnp.zeros((8, 128), F32)], axis=0)
    for k in range(N_DP):
        f_a[k] = jnp.concatenate([folded(w64, k), window(n0, k), common], axis=0).astype(BF16)
    g_a[d] = f_a[d]
    loads[0].wait()
    loads[1].wait()
    for i in (0, 1):
        share_core(i)
    all_wait(0, d_att)
    hid = [d_att[p] + d_att[p + N_MOD] for p in range(N_MOD)]
    hmu = sum(row_sum(h) for h in hid) * (1.0 / D)
    hvar = sum(row_sum((h - hmu) * (h - hmu)) for h in hid) * (1.0 / D)
    hinv = lax.rsqrt(hvar + EPSILON)
    for p in range(N_MOD):
        hn_ref[p] = (hid[p] - hmu) * hinv
    hn = jnp.concatenate([hn_ref[p] for p in range(N_MOD)], axis=1)

    hn_b = hn.astype(BF16)
    for i in (0, 1):
        complete(i)
    proj = jnp.concatenate([dot(hn_b, full(wp0_ref)), dot(hn_b, full(wp1_ref))], axis=1)
    pinv = lax.rsqrt(row_sum(proj * proj) + EPSILON)
    embed = proj * pinv
    emb = blocks(embed).astype(BF16)
    f_emb[...] = emb
    g_emb[d] = emb
    dp_start(1, whole(f_emb), g_emb)
    for i in (2, 3, 4):
        share_core(i)
    dp_wait(0, g_oth)
    other_f = unblocks(g_oth[...].astype(F32))
    other_inv = lax.rsqrt(row_sum(other_f * other_f) + EPSILON)
    unit = other_f * other_inv
    unit_ref[...] = unit
    unit_b = unit.astype(BF16)
    dp_start(2, part(f_a), g_a)
    dp_wait(1, g_emb)

    emb_b = unblocks(g_emb[...].astype(F32)).astype(BF16)
    logits = dot_nt(emb_b, unit_b) * LOGIT_SCALE
    left = lax.broadcasted_iota(jnp.int32, (ALL, ALL), 0)
    right = lax.broadcasted_iota(jnp.int32, (ALL, ALL), 1)
    paired = ((left >> 1) & 3) == ((right >> 1) & 3)
    ex = jnp.where(paired, jnp.exp(logits), 0.0)
    row_total = row_sum(ex)
    col_total = jnp.sum(ex, axis=0, keepdims=True)
    grad = (0.5 / PAIRS) * (ex / row_total + ex / col_total)
    grad = grad - jnp.where(left == right, 1.0 / PAIRS, 0.0)
    grad_ref[...] = grad
    grad8 = grad_ref[pl.ds(d * GROUP, GROUP), :].astype(BF16)
    d_embed = LOGIT_SCALE * dot(grad8, unit_b)
    d_proj = (d_embed - embed * row_sum(embed * d_embed)) * pinv
    d_proj_b = d_proj.astype(BF16)
    dh = dot_nt(d_proj_b[:, :512], full(wp0_ref)) + dot_nt(d_proj_b[:, 512:], full(wp1_ref))
    m1 = row_sum(dh) * (1.0 / D)
    m2 = row_sum(dh * hn) * (1.0 / D)
    d_hidden = hinv * (dh - m1 - hn * m2)
    complete(2)
    d_context = dot(d_hidden.astype(BF16), full(wo_ref))

    mine = own_rows(d_context)
    heads = jnp.concatenate(
        [jnp.where(mask, mine[0:1], 0.0), jnp.where(mask, mine[1:2], 0.0)], axis=0
    )
    complete(3)
    vd_b = dot_nt(heads.astype(BF16), full(wv_ref)).astype(BF16)
    d_soft = dot_nt(vd_b, xn_ref[...])
    d_score = soft * (d_soft - row_sum(soft * d_soft))
    d_score_b = d_score.astype(BF16)
    u = dot(d_score_b, xn_ref[...]) * SCALE
    complete(4)
    uk = dot(u.astype(BF16), full(wk_ref))
    dq = place(jnp.concatenate(
        [
            jnp.sum(jnp.where(mask, uk[0:8], 0.0), axis=0, keepdims=True),
            jnp.sum(jnp.where(mask, uk[8:16], 0.0), axis=0, keepdims=True),
        ],
        axis=0,
    ))
    dq = jnp.concatenate([dq[:, :SLICE], dq[:, SLICE:]], axis=0)
    for p, v in enumerate(columns(u)):
        s_u[p] = jnp.concatenate([v, dq], axis=0)
    d_u[m] = s_u[m]
    mod_start(6, part(s_u), d_u)
    s_sc[0:16] = (d_score * SCALE).astype(BF16)
    s_sc[16:32] = soft_b
    s_kv[0:16] = kq_b
    s_kv[16:32] = vd_b
    go(tp_copy(0, s_sc, d_sc))
    go(tp_copy(1, s_kv, d_kv))
    for p, v in enumerate(columns(d_hidden)):
        dhid_ref[p] = v
    hn_m, dhid_m = hn_ref[m], dhid_ref[m]
    common = jnp.concatenate(
        [blocks(d_context), blocks(d_proj), jnp.zeros((8, 128), F32)], axis=0
    )
    for k in range(N_DP):
        f_b[k] = jnp.concatenate([window(hn_m, k), window(dhid_m, k), common], axis=0).astype(
            BF16
        )
    g_b[d] = f_b[d]
    dp_start(3, part(f_b), g_b)
    mod_wait(6, d_u)
    u64 = d_u[:, 0:16].reshape(64, SLICE)
    dq = d_u[0, 16:32] + d_u[1, 16:32] + d_u[2, 16:32] + d_u[3, 16:32]
    dq = jnp.concatenate([dq[0:8], dq[8:16]], axis=1)
    common = jnp.concatenate([blocks(dq), jnp.zeros((8, 128), F32)], axis=0)
    for k in range(N_DP):
        f_c[k] = jnp.concatenate([folded(u64, k), common], axis=0).astype(BF16)
    g_c[d] = f_c[d]
    dp_start(4, part(f_c), g_c)
    cg = dot_nt(dq.astype(BF16), wq_ref[...])
    s_cg[...] = cg
    d_cg[me] = cg
    all_start(1, s_cg, d_cg)

    rows_m = ((lax.broadcasted_iota(jnp.int32, (ALL, 1), 0) >> 1) & 3) == m
    cols_m = ((lax.broadcasted_iota(jnp.int32, (1, ALL), 1) >> 1) & 3) == m
    diag = row_sum(jnp.where(left == right, logits, 0.0))
    loss = jnp.sum(
        jnp.where(rows_m, 0.5 * jnp.log(row_total) - diag, 0.0), axis=0, keepdims=True
    ) + row_sum(jnp.where(cols_m, 0.5 * jnp.log(col_total), 0.0))
    loss_ref[...] = jnp.broadcast_to(loss * (1.0 / PAIRS), (8, 128))
    d_unit = LOGIT_SCALE * dot_tn(grad.astype(BF16), emb_b)
    unit_ref[...] = (d_unit - unit * row_sum(unit * d_unit)) * other_inv
    gother_ref[...] = own_rows(unit_ref[pl.ds(d * GROUP, GROUP), :])[0:IMGS].astype(BF16)

    def spread_q(k, carry):
        spread(qbd_ref, k, unblocks(g_a[pl.ds(k, 1), 40:80].astype(F32)))
        return carry

    dp_wait(2, g_a)
    lax.fori_loop(0, N_DP, spread_q, 0)

    tp_copy(0, s_sc, d_sc).wait_recv()
    tp_copy(1, s_kv, d_kv).wait_recv()
    weights = jnp.concatenate([s_sc[...], d_sc[...]], axis=0).astype(F32).T.astype(BF16)
    factors = jnp.concatenate([s_kv[...], d_kv[...]], axis=0)
    half = pl.ds(pl.multiple_of(t * HALF, 128), HALF)
    for c in range(PAD_ROWS // CHUNK):
        at = pl.ds(c * CHUNK, CHUNK)
        dn = dot(weights[c * CHUNK : (c + 1) * CHUNK], factors)
        mu, inv = mu_ref[at, :], inv_ref[at, :]
        xh = (x_ref[at, :].astype(F32) - mu) * inv
        mean_grad = row_sum(dn) * (1.0 / D)
        mean_cross = row_sum(dn * xh) * (1.0 / D)
        dn_ref[...] = dn
        if c == 0:
            dn0_ref[...] = dn[0:8]
        xh = (x_ref[at, half].astype(F32) - mu) * inv
        grad_x = inv * (dn_ref[:, half] - mean_grad - xh * mean_cross)
        gtok_ref[pl.ds(c * CHUNK // 2, CHUNK // 2)] = grad_x.reshape(CHUNK // 2, IMGS, HALF).astype(
            BF16
        )

    all_wait(1, d_cg)
    extra = own_rows(
        jnp.concatenate([d_cg[p] + d_cg[p + N_MOD] for p in range(N_MOD)], axis=1)
    )
    dn = dn0_ref[...] + extra
    mu, inv = mu_ref[0:8, :], inv_ref[0:8, :]
    xh = (x_ref[0:16, :].astype(F32)[0:8] - mu) * inv
    mean_grad = row_sum(dn) * (1.0 / D)
    mean_cross = row_sum(dn * xh) * (1.0 / D)
    dn0_ref[...] = inv * (dn - mean_grad - xh * mean_cross) + own_rows(d_hidden)
    gtok_ref[0] = dn0_ref[:, half][0:IMGS].astype(BF16)

    def spread_c(k, carry):
        spread(dbd_ref, k, unblocks(g_b[pl.ds(k, 1), 16:56].astype(F32)))
        return carry

    dp_wait(3, g_b)
    lax.fori_loop(0, N_DP, spread_c, 0)
    gqkv_ref[2] = head_grad(g_a[:, 0:32], dbd_ref)
    early = g_a[...].astype(F32)
    late = g_b[...].astype(F32)
    hn_all = unblocks(late[:, 0:8]).astype(BF16)
    dhid_all = unblocks(late[:, 8:16]).astype(BF16)
    gproj_ref[...] = dot_tn(hn_all, unblocks(late[:, 56:120]).astype(BF16))[0:OUT_ROWS]
    gout_ref[...] = dot_tn(dhid_all, unblocks(early[:, 80:120]).astype(BF16))[0:OUT_ROWS]
    n0_all = unblocks(early[:, 32:40]).astype(BF16)
    dp_wait(4, g_c)
    gqkv_ref[1] = head_grad(g_c[:, 0:32], qbd_ref)
    dq_all = unblocks(g_c[...].astype(F32)[:, 32:72]).astype(BF16)
    gqkv_ref[0] = dot_tn(n0_all, dq_all)[0:OUT_ROWS]

    for wait in leaving:
        wait()


def store(*refs):
    sources, targets, sem = refs[:6], refs[6:12], refs[12]
    copies = [
        pltpu.make_async_copy(src, dst, sem.at[k])
        for k, (src, dst) in enumerate(
            [(sources[1].at[pl.ds(0, TOK)], targets[1])] + list(zip(sources[2:], targets[2:]))
        )
    ]
    for copy in copies:
        copy.start()
    targets[0][0] = jnp.max(sources[0][0:1, 0:1])
    for copy in copies:
        copy.wait()


def local(tokens, w_qkv, w_out, w_proj, other_emb):
    vmem = pl.BlockSpec(memory_space=pltpu.VMEM)
    hbm = pl.BlockSpec(memory_space=pltpu.HBM)

    def pair(send, land, dtype=F32):
        return [pltpu.VMEM(send, dtype), pltpu.VMEM(land, dtype)]

    def mod_all(n, k):
        return pair((n, k), (N_MOD, n, k))

    def mod_each(n):
        return pair((N_MOD, n, SLICE), (N_MOD, n, SLICE))

    def dp_all(n):
        return pair((n, 128), (N_DP, n, 128), BF16)

    def dp_each(n):
        return pair((N_DP, n, 128), (N_DP, n, 128), BF16)

    scratch = [pltpu.VMEM((IMGS, E), BF16), pltpu.VMEM((TOK, IMGS, D), BF16), pltpu.VMEM((PAD_ROWS, D), BF16)]
    scratch += [pltpu.VMEM((SLICE, HALF), BF16)]
    scratch += [pltpu.VMEM((N_MOD, SLICE, k), BF16) for k in COLUMNS]
    scratch += [
        pltpu.VMEM((PAD_ROWS, D), BF16),
        pltpu.VMEM((PAD_ROWS, 1), F32),
        pltpu.VMEM((PAD_ROWS, 1), F32),
        pltpu.VMEM((ALL, ALL), F32),
        pltpu.VMEM((CHUNK, D), F32),
        pltpu.VMEM((8, D), F32),
        pltpu.VMEM((ALL, E), F32),
        pltpu.VMEM((2, N_DP * 32, HALF), BF16),
        pltpu.VMEM((2, N_DP * 32, HALF), BF16),
        pltpu.VMEM((N_MOD, GROUP, SLICE), F32),
        pltpu.VMEM((N_MOD, GROUP, SLICE), F32),
    ]
    scratch += mod_each(16) + mod_all(8, E) + mod_all(8, HALF) + mod_each(16) + mod_each(16)
    scratch += mod_all(8, HALF) + pair((8, SLICE), (2 * N_MOD, 8, SLICE))
    scratch += mod_each(32) + pair((8, SLICE), (2 * N_MOD, 8, SLICE))
    scratch += pair((32, PAD_ROWS), (32, PAD_ROWS), BF16) + pair((32, D), (32, D), BF16)
    scratch += dp_all(64) + dp_all(64) + dp_each(128) + dp_each(128) + dp_each(80)
    dma = pltpu.SemaphoreType.DMA
    n = len(COLUMNS)
    scratch += [dma((n + 3,)), dma((n, 2)), dma((n, 2)), dma((n,)), dma((n,))]
    scratch += [dma((n,)), dma((n,)), dma((n, 2)), dma((n, 2))]
    scratch += [dma((7,)), dma((7,)), dma((2,)), dma((2,)), dma((2,)), dma((2,))]
    scratch += [dma((5,)), dma((5,))]

    def shape(*dims, dtype=F32):
        return jax.ShapeDtypeStruct(dims, dtype)

    results = pl.pallas_call(
        kernel,
        out_shape=[
            shape(8, 128),
            shape(PAD_TOK, IMGS, HALF, dtype=BF16),
            shape(3, OUT_ROWS, HALF),
            shape(OUT_ROWS, HALF),
            shape(OUT_ROWS, E),
            shape(IMGS, E, dtype=BF16),
        ],
        in_specs=[hbm] * 5,
        out_specs=[vmem] * 6,
        scratch_shapes=scratch,
        compiler_params=pltpu.CompilerParams(
            collective_id=0, has_side_effects=True, vmem_limit_bytes=48 * 2**20
        ),
    )(
        *(
            pltpu.with_memory_space_constraint(v, pltpu.HBM)
            for v in (
                tokens.transpose(1, 0, 2), w_qkv.transpose(1, 0, 2), w_out, w_proj, other_emb
            )
        )
    )
    loss, grad_tokens, grad_qkv, grad_out, grad_proj, grad_other = pl.pallas_call(
        store,
        out_shape=[
            shape(1),
            shape(TOK, IMGS, HALF, dtype=BF16),
            shape(3, OUT_ROWS, HALF),
            shape(OUT_ROWS, HALF),
            shape(OUT_ROWS, E),
            shape(IMGS, E, dtype=BF16),
        ],
        in_specs=[vmem] * 6,
        out_specs=[pl.BlockSpec(memory_space=pltpu.SMEM)] + [hbm] * 5,
        scratch_shapes=[pltpu.SemaphoreType.DMA((5,))],
        compiler_params=pltpu.CompilerParams(vmem_limit_bytes=16 * 2**20),
    )(*results)
    return (
        loss,
        grad_tokens.transpose(1, 0, 2),
        grad_qkv.transpose(1, 0, 2),
        grad_out,
        grad_proj,
        grad_other,
    )


def solution(mesh):
    placed = (
        P(("mod", "dp"), None, None),
        P("mod", None, "tp"),
        P("mod", "tp"),
        P("mod", None),
        P(("mod", "dp"), None),
    )
    return jax.shard_map(
        local,
        mesh=mesh,
        in_specs=placed,
        out_specs=(
            P("mod"),
            P(("mod", "dp"), None, "tp"),
            P(("mod", "dp"), None, "tp"),
            P(("mod", "dp"), "tp"),
            P(("mod", "dp"), None),
            P(("mod", "dp"), None),
        ),
        check_vma=False,
    )
```

time: 77.7 us -> 58.4 us (0.75)
  Pallas kernels: 67.3 us -> 57.4 us
  local copies, waits for them, and re-layouts: 9.52 us -> 0 us
    pallas_call x1 -> x2, Pallas kernels: 67.3 us -> 57.4 us  [the longest x1 55.9 us: local(): pl.pallas_call(kernel, out_shape=[shape(8, 128), shape(PAD_TOK, IMGS, HAL...]
    reshape x2 -> x0, local copies, waits for them, and re-layouts: 4.89 us -> none  [the longest x1 3.21 us: local(): rows = tokens.transpose(1, 0, 2).reshape(ROWS, D)]
    unnamed x11 -> x0, local copies, waits for them, and re-layouts: 3.38 us -> none
    slice x3 -> x0, local copies, waits for them, and re-layouts: 1.17 us -> none  [the longest x1 0.6 us: local(): grad_other[0:IMGS].astype(BF16)]
where the time goes in v2:
time: 58.4 us; the launch traced here: 58 us
  Pallas kernels  57.4 us (98%)
  between operations  0.64 us (1%)
    pallas_call x1, Pallas kernels, local(): pl.pallas_call(kernel, out_shape=[shape(8, 128), shape(PAD_TOK, IMGS, HAL...  55.9 us
    pallas_call x1, Pallas kernels, local(): pl.pallas_call(store, out_shape=[shape(1), shape(TOK, IMGS, HALF, dtype=B...  1.5 us

profile of v2, /device:TPU:1, one launch (start us, length us, event | category | flops | bytes accessed | tf_op | source)
XLA Modules:
  0.0 58.0 jit_solution(2270728903158621239)
XLA Ops:
  0.6 55.9 %shard_map.100 = (f32[8,128]{1,0:T(8,128)S(1)}, bf16[264,2,640]{2,1,0:T(2,128)(2,1)S(1)}, f32[3,20,640]{2,1,0:T(8,128)S(1)}, f32[20,640]{1,0:T(8,128)S(1)}, f32[...) custom-call(bf16[257,2,1280]{2,1,0:T(2,128)(2,1)} %bitcast.4, bf16[3,320,640]{2,1,0:T(8,128)(2,1)} %bitcast.5, ...), custom_call_target="tpu_custom_call" | custom-call | tf_op jit(solution)/shard_map/pallas_call | solution.py:684
  56.5 1.5 %shard_map.101 = (f32[1]{0:T(128)}, bf16[257,2,640]{2,1,0:T(2,128)(2,1)}, f32[3,20,640]{2,1,0:T(8,128)}, f32[20,640]{1,0:T(8,128)}, f32[20,1024]{1,0:T(8,128)}, /*index=5*/bf16[2,1024]{1,0:T(2,128)(2,1)}) custom-call(f32[8,128]{1,0:T(8,128)S(1)} %get-tuple-element.18.refs_0_, bf16[264,2,640]{2,1,0:T(2,128)(2,1)S(1)} %get-tuple-element.19.refs_1_, ...), custom_call_target="tpu_custom_call" | custom-call | tf_op jit(solution)/shard_map/pallas_call | solution.py:708

commit v3 on v2

--- a/solution.py
+++ b/solution.py
@@ -32,8 +32,12 @@
 ALL = GROUP * N_DP
 SCALE = HEAD_DIM**-0.5
 COLUMNS = (512, 512, 640, 640, 640)
-ROWS_BY_X = (True, False, False, True, True)
+ROWS_BY_X = (True, False, True, False, True)
 PIECE = SLICE // 4
+FAR_FIRST = sorted(
+    [(i, j) for i in range(4) for j in range(4) if i or j],
+    key=lambda s: -(min(s[0], 4 - s[0]) + min(s[1], 4 - s[1])),
+)
 
 
 def dot(a, b):
@@ -92,7 +96,7 @@
 def kernel(
     x_hbm, wqkv_hbm, wout_hbm, wproj_hbm, other_hbm,
     loss_ref, gtok_ref, gqkv_ref, gout_ref, gproj_ref, gother_ref,
-    other_ref, pairs_ref, x_ref, wq_ref, wp0_ref, wp1_ref, wo_ref, wv_ref, wk_ref,
+    other_ref, pairs_ref, x_ref, value_ref, wq_ref, wp0_ref, wp1_ref, wo_ref, wv_ref, wk_ref,
     xn_ref, mu_ref, inv_ref, grad_ref, dn_ref, dn0_ref, unit_ref, qbd_ref, dbd_ref, hn_ref, dhid_ref,
     s_cls, d_cls, s_oth, d_oth, s_q, d_q, s_kq, d_kq, s_w, d_w, s_ctx, d_ctx, s_att, d_att,
     s_u, d_u, s_cg, d_cg, s_sc, d_sc, s_kv, d_kv,
@@ -271,6 +275,12 @@
         lax.fori_loop(1, N_DP, body, 0)
         leaving.append(lambda: dp_all(n, dst).wait_send())
 
+    def dp_start_far(n, src, dst):
+        for i, j in FAR_FIRST:
+            peer = lax.rem(cx + i, 4) * 4 + lax.rem(cz + j, 4)
+            start(remote(src(peer), dst.at[d], dp_send.at[n], dp_recv.at[n], (m, peer, t)))
+        leaving.append(lambda: dp_all(n, dst).wait_send())
+
     def dp_wait(n, dst):
         dp_all(n, dst).wait_recv()
 
@@ -338,12 +348,12 @@
     for p, v in enumerate(columns(jnp.concatenate([place(n8), place(x8)], axis=0))):
         s_cls[p] = v
     d_cls[m] = s_cls[m]
-    oth = place(other_ref[...].astype(F32))
+    oth = blocks(place(other_ref[...].astype(F32))).astype(BF16)
     s_oth[...] = oth
     d_oth[m] = oth
     pl.semaphore_wait(barrier, N_MOD - 1 + N_MOD + N_DP - 1)
     mod_start(0, part(s_cls), d_cls)
-    for i in (0, 1):
+    for i in range(5):
         fetch_across(i)
     for i in (0, 1):
         fetch_core(i)
@@ -366,11 +376,10 @@
     s_q[...] = qp
     d_q[m] = qp
     mod_start(1, whole(s_q), d_q)
+    for i in (0, 1):
+        share_cols(i)
+    normalise(1)
     for i in (2, 3, 4):
-        fetch_across(i)
-    mod_start(2, whole(s_oth), d_oth)
-    normalise(1)
-    for i in (0, 1):
         share_cols(i)
     loads[4].wait()
     mod_wait(1, d_q)
@@ -381,12 +390,11 @@
         s_kq[p] = kq[p * 16 : (p + 1) * 16]
     d_kq[m] = s_kq[m]
     mod_start(3, part(s_kq), d_kq)
+    mod_start(2, whole(s_oth), d_oth)
     for i in (2, 3, 4):
         fetch_core(i)
     normalise(2)
-    for i in (2, 3, 4):
-        share_cols(i)
-    for i in (0, 1):
+    for i in range(5):
         share_rows(i)
     mod_wait(3, d_kq)
     kq_b = jnp.concatenate([d_kq[p] for p in range(N_MOD)], axis=1).astype(BF16)
@@ -403,13 +411,11 @@
         s_w[p] = v
     d_w[m] = s_w[m]
     mod_start(4, part(s_w), d_w)
-    for i in (2, 3, 4):
-        share_rows(i)
     mod_wait(2, d_oth)
-    oth = blocks(d_oth[0] + d_oth[1] + d_oth[2] + d_oth[3]).astype(BF16)
+    oth = d_oth[0].astype(F32) + d_oth[1].astype(F32)
+    oth = (oth + d_oth[2].astype(F32) + d_oth[3].astype(F32)).astype(BF16)
     f_oth[...] = oth
     g_oth[d] = oth
-    dp_start(0, whole(f_oth), g_oth)
     loads[3].wait()
     mod_wait(4, d_w)
     w64 = d_w[...].reshape(64, SLICE)
@@ -418,6 +424,7 @@
     s_ctx[...] = cp
     d_ctx[m] = cp
     mod_start(5, whole(s_ctx), d_ctx)
+    dp_start(0, whole(f_oth), g_oth)
     loads[2].wait()
     mod_wait(5, d_ctx)
     ctx = d_ctx[0] + d_ctx[1] + d_ctx[2] + d_ctx[3]
@@ -426,10 +433,6 @@
     s_att[...] = ap
     d_att[me] = ap
     all_start(0, s_att, d_att)
-    common = jnp.concatenate([blocks(q), blocks(ctx), jnp.zeros((8, 128), F32)], axis=0)
-    for k in range(N_DP):
-        f_a[k] = jnp.concatenate([folded(w64, k), window(n0, k), common], axis=0).astype(BF16)
-    g_a[d] = f_a[d]
     loads[0].wait()
     loads[1].wait()
     for i in (0, 1):
@@ -452,9 +455,16 @@
     emb = blocks(embed).astype(BF16)
     f_emb[...] = emb
     g_emb[d] = emb
-    dp_start(1, whole(f_emb), g_emb)
-    for i in (2, 3, 4):
+    dp_start_far(1, whole(f_emb), g_emb)
+    for i in (3, 2, 4):
         share_core(i)
+    hn_m = hn_ref[m]
+    common = jnp.concatenate([blocks(q), blocks(ctx)], axis=0)
+    for k in range(N_DP):
+        f_a[k] = jnp.concatenate(
+            [folded(w64, k), window(n0, k), window(hn_m, k), common], axis=0
+        ).astype(BF16)
+    g_a[d] = f_a[d]
     dp_wait(0, g_oth)
     other_f = unblocks(g_oth[...].astype(F32))
     other_inv = lax.rsqrt(row_sum(other_f * other_f) + EPSILON)
@@ -462,6 +472,10 @@
     unit_ref[...] = unit
     unit_b = unit.astype(BF16)
     dp_start(2, part(f_a), g_a)
+    complete(3)
+    for c in range(PAD_ROWS // CHUNK):
+        at = pl.ds(c * CHUNK, CHUNK)
+        value_ref[at, :] = dot(xn_ref[at, :], full(wv_ref)).astype(BF16)
     dp_wait(1, g_emb)
 
     emb_b = unblocks(g_emb[...].astype(F32)).astype(BF16)
@@ -489,10 +503,8 @@
     mine = own_rows(d_context)
     heads = jnp.concatenate(
         [jnp.where(mask, mine[0:1], 0.0), jnp.where(mask, mine[1:2], 0.0)], axis=0
-    )
-    complete(3)
-    vd_b = dot_nt(heads.astype(BF16), full(wv_ref)).astype(BF16)
-    d_soft = dot_nt(vd_b, xn_ref[...])
+    ).astype(BF16)
+    d_soft = dot_nt(heads, value_ref[...])
     d_score = soft * (d_soft - row_sum(soft * d_soft))
     d_score_b = d_score.astype(BF16)
     u = dot(d_score_b, xn_ref[...]) * SCALE
@@ -510,6 +522,7 @@
         s_u[p] = jnp.concatenate([v, dq], axis=0)
     d_u[m] = s_u[m]
     mod_start(6, part(s_u), d_u)
+    vd_b = dot_nt(heads, full(wv_ref)).astype(BF16)
     s_sc[0:16] = (d_score * SCALE).astype(BF16)
     s_sc[16:32] = soft_b
     s_kv[0:16] = kq_b
@@ -518,14 +531,15 @@
     go(tp_copy(1, s_kv, d_kv))
     for p, v in enumerate(columns(d_hidden)):
         dhid_ref[p] = v
-    hn_m, dhid_m = hn_ref[m], dhid_ref[m]
+    dhid_m = dhid_ref[m]
+    high = pinv.astype(BF16).astype(F32)
+    lane = lax.broadcasted_iota(jnp.int32, (GROUP, 128), 1)
     common = jnp.concatenate(
-        [blocks(d_context), blocks(d_proj), jnp.zeros((8, 128), F32)], axis=0
+        [jnp.where(lane < 64, high, pinv - high), blocks(d_context), jnp.zeros((8, 128), F32)],
+        axis=0,
     )
     for k in range(N_DP):
-        f_b[k] = jnp.concatenate([window(hn_m, k), window(dhid_m, k), common], axis=0).astype(
-            BF16
-        )
+        f_b[k] = jnp.concatenate([window(dhid_m, k), common], axis=0).astype(BF16)
     g_b[d] = f_b[d]
     dp_start(3, part(f_b), g_b)
     mod_wait(6, d_u)
@@ -536,7 +550,7 @@
     for k in range(N_DP):
         f_c[k] = jnp.concatenate([folded(u64, k), common], axis=0).astype(BF16)
     g_c[d] = f_c[d]
-    dp_start(4, part(f_c), g_c)
+    dp_start_far(4, part(f_c), g_c)
     cg = dot_nt(dq.astype(BF16), wq_ref[...])
     s_cg[...] = cg
     d_cg[me] = cg
@@ -554,7 +568,7 @@
     gother_ref[...] = own_rows(unit_ref[pl.ds(d * GROUP, GROUP), :])[0:IMGS].astype(BF16)
 
     def spread_q(k, carry):
-        spread(qbd_ref, k, unblocks(g_a[pl.ds(k, 1), 40:80].astype(F32)))
+        spread(qbd_ref, k, unblocks(g_a[pl.ds(k, 1), 48:88].astype(F32)))
         return carry
 
     dp_wait(2, g_a)
@@ -602,10 +616,15 @@
     gqkv_ref[2] = head_grad(g_a[:, 0:32], dbd_ref)
     early = g_a[...].astype(F32)
     late = g_b[...].astype(F32)
-    hn_all = unblocks(late[:, 0:8]).astype(BF16)
-    dhid_all = unblocks(late[:, 8:16]).astype(BF16)
-    gproj_ref[...] = dot_tn(hn_all, unblocks(late[:, 56:120]).astype(BF16))[0:OUT_ROWS]
-    gout_ref[...] = dot_tn(dhid_all, unblocks(early[:, 80:120]).astype(BF16))[0:OUT_ROWS]
+    dhid_all = unblocks(late[:, 0:8]).astype(BF16)
+    gout_ref[...] = dot_tn(dhid_all, unblocks(early[:, 88:128]).astype(BF16))[0:OUT_ROWS]
+    pinv_all = unblocks(late[:, 8:16])
+    pinv_all = pinv_all[:, 0:1] + pinv_all[:, 64:65]
+    emb = emb_b.astype(F32)
+    d_embed = LOGIT_SCALE * dot(grad.astype(BF16), unit_b)
+    d_proj = (d_embed - emb * row_sum(emb * d_embed)) * pinv_all
+    hn_all = unblocks(early[:, 40:48]).astype(BF16)
+    gproj_ref[...] = dot_tn(hn_all, d_proj.astype(BF16))[0:OUT_ROWS]
     n0_all = unblocks(early[:, 32:40]).astype(BF16)
     dp_wait(4, g_c)
     gqkv_ref[1] = head_grad(g_c[:, 0:32], qbd_ref)
@@ -651,6 +670,7 @@
         return pair((N_DP, n, 128), (N_DP, n, 128), BF16)
 
     scratch = [pltpu.VMEM((IMGS, E), BF16), pltpu.VMEM((TOK, IMGS, D), BF16), pltpu.VMEM((PAD_ROWS, D), BF16)]
+    scratch += [pltpu.VMEM((PAD_ROWS, HALF), BF16)]
     scratch += [pltpu.VMEM((SLICE, HALF), BF16)]
     scratch += [pltpu.VMEM((N_MOD, SLICE, k), BF16) for k in COLUMNS]
     scratch += [
@@ -666,11 +686,11 @@
         pltpu.VMEM((N_MOD, GROUP, SLICE), F32),
         pltpu.VMEM((N_MOD, GROUP, SLICE), F32),
     ]
-    scratch += mod_each(16) + mod_all(8, E) + mod_all(8, HALF) + mod_each(16) + mod_each(16)
+    scratch += mod_each(16) + pair((64, 128), (N_MOD, 64, 128), BF16) + mod_all(8, HALF) + mod_each(16) + mod_each(16)
     scratch += mod_all(8, HALF) + pair((8, SLICE), (2 * N_MOD, 8, SLICE))
     scratch += mod_each(32) + pair((8, SLICE), (2 * N_MOD, 8, SLICE))
     scratch += pair((32, PAD_ROWS), (32, PAD_ROWS), BF16) + pair((32, D), (32, D), BF16)
-    scratch += dp_all(64) + dp_all(64) + dp_each(128) + dp_each(128) + dp_each(80)
+    scratch += dp_all(64) + dp_all(64) + dp_each(128) + dp_each(64) + dp_each(80)
     dma = pltpu.SemaphoreType.DMA
     n = len(COLUMNS)
     scratch += [dma((n + 3,)), dma((n, 2)), dma((n, 2)), dma((n,)), dma((n,))]

time: 58.4 us -> 54.8 us (0.938)
  Pallas kernels: 57.4 us -> 54 us
    pallas_call x1, Pallas kernels: 55.9 us -> 52.5 us  [local(): pl.pallas_call(kernel, out_shape=[shape(8, 128), shape(PAD_TOK, IMGS, HAL...]
where the time goes in v3:
time: 54.8 us; the launch traced here: 54.7 us
  Pallas kernels  54 us (99%)
  between operations  0.64 us (1%)
    pallas_call x1, Pallas kernels, local(): pl.pallas_call(kernel, out_shape=[shape(8, 128), shape(PAD_TOK, IMGS, HAL...  52.5 us
    pallas_call x1, Pallas kernels, local(): pl.pallas_call(store, out_shape=[shape(1), shape(TOK, IMGS, HALF, dtype=B...  1.5 us

profile of v3, /device:TPU:1, one launch (start us, length us, event | category | flops | bytes accessed | tf_op | source)
XLA Modules:
  0.0 54.7 jit_solution(17514212471938371533)
XLA Ops:
  0.6 52.5 %shard_map.100 = (f32[8,128]{1,0:T(8,128)S(1)}, bf16[264,2,640]{2,1,0:T(2,128)(2,1)S(1)}, f32[3,20,640]{2,1,0:T(8,128)S(1)}, f32[20,640]{1,0:T(8,128)S(1)}, f32[...) custom-call(bf16[257,2,1280]{2,1,0:T(2,128)(2,1)} %bitcast.4, bf16[3,320,640]{2,1,0:T(8,128)(2,1)} %bitcast.5, ...), custom_call_target="tpu_custom_call" | custom-call | tf_op jit(solution)/shard_map/pallas_call | solution.py:704
  53.2 1.5 %shard_map.101 = (f32[1]{0:T(128)}, bf16[257,2,640]{2,1,0:T(2,128)(2,1)}, f32[3,20,640]{2,1,0:T(8,128)}, f32[20,640]{1,0:T(8,128)}, f32[20,1024]{1,0:T(8,128)}, /*index=5*/bf16[2,1024]{1,0:T(2,128)(2,1)}) custom-call(f32[8,128]{1,0:T(8,128)S(1)} %get-tuple-element.18.refs_0_, bf16[264,2,640]{2,1,0:T(2,128)(2,1)S(1)} %get-tuple-element.19.refs_1_, ...), custom_call_target="tpu_custom_call" | custom-call | tf_op jit(solution)/shard_map/pallas_call | solution.py:728

commit v4 on v3

--- a/solution.py
+++ b/solution.py
@@ -321,17 +321,19 @@
     def folded(v, k):
         wide = jnp.concatenate([v, jnp.zeros((64, 64), F32)], axis=1)
         at = k * OUT_ROWS
-        return jnp.concatenate([wide[0:32, at : at + 64], wide[32:64, at : at + 64]], axis=1)
+        return jnp.concatenate([wide[r : r + 16, at : at + 32] for r in range(0, 64, 16)], axis=1)
 
     def spread(dst, k, v):
         v = expand_heads(v, mask)
-        at = pl.ds(pl.multiple_of(k * 32, 32), 32)
-        dst[0, at, :] = v[0:32]
-        dst[1, at, :] = v[32:64]
+        at = pl.ds(pl.multiple_of(k * 16, 16), 16)
+        for r in range(4):
+            dst[r, at, :] = v[r * 16 : (r + 1) * 16]
 
     def head_grad(factor, dst):
-        factor = factor.reshape(N_DP * 32, 128)
-        return dot_tn(factor, dst[0])[0:OUT_ROWS] + dot_tn(factor, dst[1])[64 : 64 + OUT_ROWS]
+        factor = factor.reshape(N_DP * 16, 128)
+        return sum(
+            dot_tn(factor, dst[r])[r * 32 : r * 32 + OUT_ROWS] for r in range(4)
+        )
 
     def columns(v):
         return [v[:, p * SLICE : (p + 1) * SLICE] for p in range(N_MOD)]
@@ -346,7 +348,7 @@
     c8 = x8 - mu8
     n8 = c8 * lax.rsqrt(row_sum(c8 * c8) * (1.0 / D) + EPSILON)
     for p, v in enumerate(columns(jnp.concatenate([place(n8), place(x8)], axis=0))):
-        s_cls[p] = v
+        s_cls[p] = v.astype(BF16)
     d_cls[m] = s_cls[m]
     oth = blocks(place(other_ref[...].astype(F32))).astype(BF16)
     s_oth[...] = oth
@@ -369,7 +371,7 @@
     normalise(0)
     load_q.wait()
     mod_wait(0, d_cls)
-    cls = d_cls[0] + d_cls[1] + d_cls[2] + d_cls[3]
+    cls = sum(d_cls[p].astype(F32) for p in range(N_MOD))
     n0, x0 = cls[0:8], cls[8:16]
 
     qp = dot(n0.astype(BF16), wq_ref[...])
@@ -387,7 +389,7 @@
 
     kq = dot_nt(expand_heads(q, mask), wk_ref[m])
     for p in range(N_MOD):
-        s_kq[p] = kq[p * 16 : (p + 1) * 16]
+        s_kq[p] = kq[p * 16 : (p + 1) * 16].astype(BF16)
     d_kq[m] = s_kq[m]
     mod_start(3, part(s_kq), d_kq)
     mod_start(2, whole(s_oth), d_oth)
@@ -397,7 +399,7 @@
     for i in range(5):
         share_rows(i)
     mod_wait(3, d_kq)
-    kq_b = jnp.concatenate([d_kq[p] for p in range(N_MOD)], axis=1).astype(BF16)
+    kq_b = jnp.concatenate([d_kq[p].astype(F32) for p in range(N_MOD)], axis=1).astype(BF16)
 
     scores = dot_nt(kq_b, xn_ref[...]) * SCALE
     lane = lax.broadcasted_iota(jnp.int32, (16, PAD_ROWS), 1)
@@ -408,7 +410,7 @@
     soft_b = soft.astype(BF16)
     w = dot(soft_b, xn_ref[...])
     for p, v in enumerate(columns(w)):
-        s_w[p] = v
+        s_w[p] = v.astype(BF16)
     d_w[m] = s_w[m]
     mod_start(4, part(s_w), d_w)
     mod_wait(2, d_oth)
@@ -418,7 +420,7 @@
     g_oth[d] = oth
     loads[3].wait()
     mod_wait(4, d_w)
-    w64 = d_w[...].reshape(64, SLICE)
+    w64 = d_w[...].astype(F32).reshape(64, SLICE)
 
     cp = collapse_heads(dot(w64.astype(BF16), wv_ref[m]), mask)
     s_ctx[...] = cp
@@ -519,7 +521,7 @@
     ))
     dq = jnp.concatenate([dq[:, :SLICE], dq[:, SLICE:]], axis=0)
     for p, v in enumerate(columns(u)):
-        s_u[p] = jnp.concatenate([v, dq], axis=0)
+        s_u[p] = jnp.concatenate([v, dq], axis=0).astype(BF16)
     d_u[m] = s_u[m]
     mod_start(6, part(s_u), d_u)
     vd_b = dot_nt(heads, full(wv_ref)).astype(BF16)
@@ -543,8 +545,9 @@
     g_b[d] = f_b[d]
     dp_start(3, part(f_b), g_b)
     mod_wait(6, d_u)
-    u64 = d_u[:, 0:16].reshape(64, SLICE)
-    dq = d_u[0, 16:32] + d_u[1, 16:32] + d_u[2, 16:32] + d_u[3, 16:32]
+    ud = d_u[...].astype(F32)
+    u64 = ud[:, 0:16].reshape(64, SLICE)
+    dq = ud[0, 16:32] + ud[1, 16:32] + ud[2, 16:32] + ud[3, 16:32]
     dq = jnp.concatenate([dq[0:8], dq[8:16]], axis=1)
     common = jnp.concatenate([blocks(dq), jnp.zeros((8, 128), F32)], axis=0)
     for k in range(N_DP):
@@ -568,7 +571,7 @@
     gother_ref[...] = own_rows(unit_ref[pl.ds(d * GROUP, GROUP), :])[0:IMGS].astype(BF16)
 
     def spread_q(k, carry):
-        spread(qbd_ref, k, unblocks(g_a[pl.ds(k, 1), 48:88].astype(F32)))
+        spread(qbd_ref, k, unblocks(g_a[pl.ds(k, 1), 32:72].astype(F32)))
         return carry
 
     dp_wait(2, g_a)
@@ -613,22 +616,22 @@
 
     dp_wait(3, g_b)
     lax.fori_loop(0, N_DP, spread_c, 0)
-    gqkv_ref[2] = head_grad(g_a[:, 0:32], dbd_ref)
+    gqkv_ref[2] = head_grad(g_a[:, 0:16], dbd_ref)
     early = g_a[...].astype(F32)
     late = g_b[...].astype(F32)
     dhid_all = unblocks(late[:, 0:8]).astype(BF16)
-    gout_ref[...] = dot_tn(dhid_all, unblocks(early[:, 88:128]).astype(BF16))[0:OUT_ROWS]
+    gout_ref[...] = dot_tn(dhid_all, unblocks(early[:, 72:112]).astype(BF16))[0:OUT_ROWS]
     pinv_all = unblocks(late[:, 8:16])
     pinv_all = pinv_all[:, 0:1] + pinv_all[:, 64:65]
     emb = emb_b.astype(F32)
     d_embed = LOGIT_SCALE * dot(grad.astype(BF16), unit_b)
     d_proj = (d_embed - emb * row_sum(emb * d_embed)) * pinv_all
-    hn_all = unblocks(early[:, 40:48]).astype(BF16)
+    hn_all = unblocks(early[:, 24:32]).astype(BF16)
     gproj_ref[...] = dot_tn(hn_all, d_proj.astype(BF16))[0:OUT_ROWS]
-    n0_all = unblocks(early[:, 32:40]).astype(BF16)
+    n0_all = unblocks(early[:, 16:24]).astype(BF16)
     dp_wait(4, g_c)
-    gqkv_ref[1] = head_grad(g_c[:, 0:32], qbd_ref)
-    dq_all = unblocks(g_c[...].astype(F32)[:, 32:72]).astype(BF16)
+    gqkv_ref[1] = head_grad(g_c[:, 0:16], qbd_ref)
+    dq_all = unblocks(g_c[...].astype(F32)[:, 16:56]).astype(BF16)
     gqkv_ref[0] = dot_tn(n0_all, dq_all)[0:OUT_ROWS]
 
     for wait in leaving:
@@ -661,7 +664,7 @@
         return pair((n, k), (N_MOD, n, k))
 
     def mod_each(n):
-        return pair((N_MOD, n, SLICE), (N_MOD, n, SLICE))
+        return pair((N_MOD, n, SLICE), (N_MOD, n, SLICE), BF16)
 
     def dp_all(n):
         return pair((n, 128), (N_DP, n, 128), BF16)
@@ -681,8 +684,8 @@
         pltpu.VMEM((CHUNK, D), F32),
         pltpu.VMEM((8, D), F32),
         pltpu.VMEM((ALL, E), F32),
-        pltpu.VMEM((2, N_DP * 32, HALF), BF16),
-        pltpu.VMEM((2, N_DP * 32, HALF), BF16),
+        pltpu.VMEM((4, N_DP * 16, HALF), BF16),
+        pltpu.VMEM((4, N_DP * 16, HALF), BF16),
         pltpu.VMEM((N_MOD, GROUP, SLICE), F32),
         pltpu.VMEM((N_MOD, GROUP, SLICE), F32),
     ]
@@ -690,7 +693,7 @@
     scratch += mod_all(8, HALF) + pair((8, SLICE), (2 * N_MOD, 8, SLICE))
     scratch += mod_each(32) + pair((8, SLICE), (2 * N_MOD, 8, SLICE))
     scratch += pair((32, PAD_ROWS), (32, PAD_ROWS), BF16) + pair((32, D), (32, D), BF16)
-    scratch += dp_all(64) + dp_all(64) + dp_each(128) + dp_each(64) + dp_each(80)
+    scratch += dp_all(64) + dp_all(64) + dp_each(112) + dp_each(64) + dp_each(64)
     dma = pltpu.SemaphoreType.DMA
     n = len(COLUMNS)
     scratch += [dma((n + 3,)), dma((n, 2)), dma((n, 2)), dma((n,)), dma((n,))]

time: 54.8 us -> 52.4 us (0.956)
  Pallas kernels: 54 us -> 51.6 us
    pallas_call x1, Pallas kernels: 52.5 us -> 50.1 us  [local(): pl.pallas_call(kernel, out_shape=[shape(8, 128), shape(PAD_TOK, IMGS, HAL...]
where the time goes in v4:
time: 52.4 us; the launch traced here: 52.3 us
  Pallas kernels  51.6 us (98%)
  between operations  0.64 us (1%)
    pallas_call x1, Pallas kernels, local(): pl.pallas_call(kernel, out_shape=[shape(8, 128), shape(PAD_TOK, IMGS, HAL...  50.1 us
    pallas_call x1, Pallas kernels, local(): pl.pallas_call(store, out_shape=[shape(1), shape(TOK, IMGS, HALF, dtype=B...  1.5 us

profile of v4, /device:TPU:1, one launch (start us, length us, event | category | flops | bytes accessed | tf_op | source)
XLA Modules:
  0.0 52.3 jit_solution(3024073991707620972)
XLA Ops:
  0.6 50.1 %shard_map.100 = (f32[8,128]{1,0:T(8,128)S(1)}, bf16[264,2,640]{2,1,0:T(2,128)(2,1)S(1)}, f32[3,20,640]{2,1,0:T(8,128)S(1)}, f32[20,640]{1,0:T(8,128)S(1)}, f32[...) custom-call(bf16[257,2,1280]{2,1,0:T(2,128)(2,1)} %bitcast.4, bf16[3,320,640]{2,1,0:T(8,128)(2,1)} %bitcast.5, ...), custom_call_target="tpu_custom_call" | custom-call | tf_op jit(solution)/shard_map/pallas_call | solution.py:707
  50.8 1.5 %shard_map.101 = (f32[1]{0:T(128)}, bf16[257,2,640]{2,1,0:T(2,128)(2,1)}, f32[3,20,640]{2,1,0:T(8,128)}, f32[20,640]{1,0:T(8,128)}, f32[20,1024]{1,0:T(8,128)}, /*index=5*/bf16[2,1024]{1,0:T(2,128)(2,1)}) custom-call(f32[8,128]{1,0:T(8,128)S(1)} %get-tuple-element.18.refs_0_, bf16[264,2,640]{2,1,0:T(2,128)(2,1)S(1)} %get-tuple-element.19.refs_1_, ...), custom_call_target="tpu_custom_call" | custom-call | tf_op jit(solution)/shard_map/pallas_call | solution.py:731

commit v5 on v4

--- a/solution.py
+++ b/solution.py
@@ -179,39 +179,39 @@
         return along_z if ROWS_BY_X[i] else along_x
 
     def pieces(i):
-        yield 0, cols_of(i, 0)
+        yield cols_of(i, 0)
         if COLUMNS[i] == 640:
-            yield 1, pl.ds(512, 128)
+            yield pl.ds(512, 128)
 
     def fetch_core(i):
-        go(remote(
-            sources[i], gathered[i].at[m], core_send.at[i, 0], core_recv.at[i, 0], (sibling, d, t)
+        start(remote(
+            sources[i], gathered[i].at[m], core_send.at[i], core_recv.at[i, 0], (sibling, d, t)
         ))
 
     def fetch_across(i):
-        for n, cols in pieces(i):
-            go(remote(
+        for cols in pieces(i):
+            start(remote(
                 sources[i].at[rows_of(i, 0), cols], gathered[i].at[m, rows_of(i, 0), cols],
-                y_send.at[i, n], y_recv.at[i, n], (across, d, t),
+                y_send, y_recv.at[i], (across, d, t),
             ))
 
     def share_cols(i):
-        for n, cols in pieces(i):
-            part_ref = gathered[i].at[across, rows_of(i, 0), cols]
-            remote(
-                part_ref, part_ref, y_send.at[i, n], y_recv.at[i, n], (across, d, t)
-            ).wait_recv()
+        wide = 256 if COLUMNS[i] == 640 else 128
+        landed = gathered[i].at[across, pl.ds(0, PIECE), pl.ds(0, wide)]
+        remote(landed, landed, y_send, y_recv.at[i], (across, d, t)).wait_recv()
         part_ref = gathered[i].at[across, rows_of(i, 0), cols_of(i, 0)]
         for k in (2, 1, 3):
-            start(remote(part_ref, part_ref, b_send.at[i], b_recv.at[i], col_peer(i, k)))
-        three = gathered[i].at[across, pl.ds(0, PIECE), pl.ds(0, 384)]
-        leaving.append(
-            remote(three, three, b_send.at[i], b_recv.at[i], col_peer(i, 1)).wait_send
-        )
+            start(remote(part_ref, part_ref, b_send, b_recv.at[i], col_peer(i, k)))
+
+    def pieces_left():
+        sent = wo_ref.at[across, pl.ds(0, 160), pl.ds(0, 512)]
+        leaving.append(remote(sent, sent, y_send, y_recv.at[0], (across, d, t)).wait_send)
+        sent = wo_ref.at[across, pl.ds(0, 240)]
+        leaving.append(remote(sent, sent, b_send, b_recv.at[0], col_peer(0, 1)).wait_send)
 
     def share_rows(i):
         three = gathered[i].at[across, pl.ds(0, PIECE), pl.ds(0, 384)]
-        remote(three, three, b_send.at[i], b_recv.at[i], col_peer(i, 1)).wait_recv()
+        remote(three, three, b_send, b_recv.at[i], col_peer(i, 1)).wait_recv()
         part_ref = gathered[i].at[across, rows_of(i, 0)]
         for k in (2, 1, 3):
             start(remote(part_ref, part_ref, a_send.at[i], a_recv.at[i], row_peer(i, k)))
@@ -224,13 +224,17 @@
         three = gathered[i].at[across, pl.ds(0, 3 * PIECE)]
         remote(three, three, a_send.at[i], a_recv.at[i], row_peer(i, 1)).wait_recv()
         block = gathered[i].at[across]
-        go(remote(block, block, core_send.at[i, 1], core_recv.at[i, 1], (sibling, d, t)))
+        start(remote(block, block, core_send.at[i], core_recv.at[i, 1], (sibling, d, t)))
+        two = gathered[i].at[pl.ds(0, 2)]
+        leaving.append(
+            remote(two, two, core_send.at[i], core_recv.at[i, 1], (sibling, d, t)).wait_send
+        )
 
     def complete(i):
         for n, owner in ((0, sibling), (1, lax.rem(sibling + 2, N_MOD))):
             block = gathered[i].at[owner]
             remote(
-                block, block, core_send.at[i, n], core_recv.at[i, n], (sibling, d, t)
+                block, block, core_send.at[i], core_recv.at[i, n], (sibling, d, t)
             ).wait_recv()
 
     def arrivals(dst, count, send, recv, peer):
@@ -383,6 +387,7 @@
     normalise(1)
     for i in (2, 3, 4):
         share_cols(i)
+    pieces_left()
     loads[4].wait()
     mod_wait(1, d_q)
     q = (d_q[0] + d_q[1] + d_q[2] + d_q[3]).astype(BF16).astype(F32)
@@ -629,6 +634,9 @@
     hn_all = unblocks(early[:, 24:32]).astype(BF16)
     gproj_ref[...] = dot_tn(hn_all, d_proj.astype(BF16))[0:OUT_ROWS]
     n0_all = unblocks(early[:, 16:24]).astype(BF16)
+    for wait in leaving[:-2]:
+        wait()
+    del leaving[:-2]
     dp_wait(4, g_c)
     gqkv_ref[1] = head_grad(g_c[:, 0:16], qbd_ref)
     dq_all = unblocks(g_c[...].astype(F32)[:, 16:56]).astype(BF16)
@@ -696,8 +704,8 @@
     scratch += dp_all(64) + dp_all(64) + dp_each(112) + dp_each(64) + dp_each(64)
     dma = pltpu.SemaphoreType.DMA
     n = len(COLUMNS)
-    scratch += [dma((n + 3,)), dma((n, 2)), dma((n, 2)), dma((n,)), dma((n,))]
-    scratch += [dma((n,)), dma((n,)), dma((n, 2)), dma((n, 2))]
+    scratch += [dma((n + 3,)), dma, dma((n,)), dma, dma((n,))]
+    scratch += [dma((n,)), dma((n,)), dma((n,)), dma((n, 2))]
     scratch += [dma((7,)), dma((7,)), dma((2,)), dma((2,)), dma((2,)), dma((2,))]
     scratch += [dma((5,)), dma((5,))]
 

time: 52.4 us -> 52.2 us (level)
  no operation moved by 1% of the time
where the time goes in v5:
time: 52.2 us; the launch traced here: 52 us
  Pallas kernels  51.4 us (98%)
  between operations  0.64 us (1%)
    pallas_call x1, Pallas kernels, local(): pl.pallas_call(kernel, out_shape=[shape(8, 128), shape(PAD_TOK, IMGS, HAL...  49.9 us
    pallas_call x1, Pallas kernels, local(): pl.pallas_call(store, out_shape=[shape(1), shape(TOK, IMGS, HALF, dtype=B...  1.5 us

profile of v5, /device:TPU:1, one launch (start us, length us, event | category | flops | bytes accessed | tf_op | source)
XLA Modules:
  0.0 52.0 jit_solution(16960199345847525529)
XLA Ops:
  0.6 49.9 %shard_map.100 = (f32[8,128]{1,0:T(8,128)S(1)}, bf16[264,2,640]{2,1,0:T(2,128)(2,1)S(1)}, f32[3,20,640]{2,1,0:T(8,128)S(1)}, f32[20,640]{1,0:T(8,128)S(1)}, f32[...) custom-call(bf16[257,2,1280]{2,1,0:T(2,128)(2,1)} %bitcast.4, bf16[3,320,640]{2,1,0:T(8,128)(2,1)} %bitcast.5, ...), custom_call_target="tpu_custom_call" | custom-call | tf_op jit(solution)/shard_map/pallas_call | solution.py:715
  50.5 1.5 %shard_map.101 = (f32[1]{0:T(128)}, bf16[257,2,640]{2,1,0:T(2,128)(2,1)}, f32[3,20,640]{2,1,0:T(8,128)}, f32[20,640]{1,0:T(8,128)}, f32[20,1024]{1,0:T(8,128)}, /*index=5*/bf16[2,1024]{1,0:T(2,128)(2,1)}) custom-call(f32[8,128]{1,0:T(8,128)S(1)} %get-tuple-element.18.refs_0_, bf16[264,2,640]{2,1,0:T(2,128)(2,1)S(1)} %get-tuple-element.19.refs_1_, ...), custom_call_target="tpu_custom_call" | custom-call | tf_op jit(solution)/shard_map/pallas_call | solution.py:739
